TPU v7x, 512 devices: a whole 4x8x8 slice. The times are simulated.
512 devices in a mesh: ctx: 32 (over y, z_lo), head: 16 (over x, z_hi, core).
Axes of the slice: x: 4, y: 8, z: 8 (z_hi: 2, z_lo: 4; z = z_hi * 4 + z_lo), core: 2. Of those that a mesh axis runs over, the one named last changes fastest.
Arguments:
- queries: bfloat16 [2, 512, 4096], P(None, ('ctx', 'head')), may hold values from -40 to 40
- cache_kv: bfloat16 [32, 2, 512, 4096], P('ctx', None, None, 'head'), may hold values from -24 to 24
- lengths: int32 [32], P('ctx'), may hold values from 64 to 512, as said below
- evict: int32 [1], replicated, may hold values from 0 to 31
- own_kv: bfloat16 [2, 2, 512, 4096], P(None, None, 'ctx', 'head'), may hold values from -6 to 6
- clean_kv: bfloat16 [2, 512, 4096], P(None, 'ctx', 'head'), may hold values from -6 to 6
Outputs:
- attended: bfloat16 [2, 512, 4096], P(None, ('ctx', 'head'))
- new_cache: bfloat16 [32, 2, 512, 4096], P('ctx', None, None, 'head')
Inputs may be any that keep to these rules, and one draw needn't show every extreme that they name: `lengths`: at least one slot is full.
All inputs are finite; a program needn't handle non-finite values.
Results may differ from a plain program's by a relative error of at most 0.0065.
Values may be sent and summed in bfloat16 or wider, within the bound.
No kernel may reach another device: no remote copies, remote signals or barrier semaphores. Data moves between devices by JAX's collectives and lax.ppermute only.
A program may use at most 64 MiB of HBM per device.

v0:
```python
import math

import jax
import jax.numpy as jnp
from jax import lax
from jax.experimental import pallas as pl
from jax.experimental.pallas import tpu as pltpu
from jax.sharding import PartitionSpec as P

HD = 128
PARTS = 8
BACK = 10
EXP2_SCALE = math.log2(math.e) / math.sqrt(HD)
NEG = -1e30
VMEM = pl.BlockSpec(memory_space=pltpu.VMEM)
SMEM = pl.BlockSpec(memory_space=pltpu.SMEM)
HBM = pl.BlockSpec(memory_space=pltpu.HBM)
NT = (((1,), (1,)), ((), ()))
NN = (((1,), (0,)), ((), ()))


def spread_kernel(q_ref, clean_ref, out_ref, copies_ref, rows):
    count = rows.shape[0]
    for row in range(count):
        chip, step, head = row // PARTS, row // 4 % 2, row % 4
        start = (chip * 4 + head) * HD
        rows[row:row + 1, :] = q_ref[step:step + 1, start:start + HD].astype(jnp.float32)
    message = rows[...].astype(out_ref.dtype)
    for dest in range(out_ref.shape[0] // count):
        out_ref[dest * count:(dest + 1) * count, :] = message
        copies_ref[dest] = clean_ref[...]


def pack_kernel(length_ref, cache_ref, own_ref, clean_ref, pack_ref, digit_rows, sems):
    span, rows = cache_ref.shape[2], clean_ref.shape[1]
    pieces = [(cache_ref.at[0, index], span) for index in range(2)]
    pieces += [(own_ref.at[step, index], rows) for step in range(2) for index in range(2)]
    pieces += [(clean_ref.at[index], rows) for index in range(2)]
    pieces += [(digit_rows, rows)]
    length = length_ref[0]
    lane = lax.broadcasted_iota(jnp.int32, (rows, 2 * HD), 1)
    digits = jnp.where(lane < HD, length // 8, length % 8)
    digit_rows[...] = digits.astype(jnp.float32).astype(digit_rows.dtype)
    place, copies = 0, []
    for number, (piece, count) in enumerate(pieces):
        copies.append(pltpu.make_async_copy(piece, pack_ref.at[pl.ds(place, count)], sems.at[number]))
        copies[-1].start()
        place += count
    for copy in copies:
        copy.wait()


def attend_kernel(evict_ref, recv_ref, pack_ref, far_ref, side_ref, cross_ref, out_ref, wide, wide_out):
    block = recv_ref.shape[0] // PARTS
    rows = 16
    span = (pack_ref.shape[0] - 7 * rows) // 2
    tail = 2 * span
    me = lax.axis_index("ca") * 2 + lax.axis_index("cb")
    core = lax.axis_index("hb")
    owners = [me == evict_ref[0], (me ^ 1) == evict_ref[0]]
    wide[...] = recv_ref[...].astype(jnp.float32)
    key = lax.broadcasted_iota(jnp.int32, (1, span), 1).astype(jnp.float32)
    lane = lax.broadcasted_iota(jnp.int32, (1, HD), 1)
    lengths = []
    for ref in (pack_ref, far_ref):
        digits = ref[tail + 6 * rows:tail + 7 * rows, :].astype(jnp.float32)[0:1]
        lengths.append(jnp.concatenate([digits[:, :HD] * 8.0 + digits[:, HD:]] * (span // HD), axis=1))
    ones = jnp.ones((span, HD), jnp.bfloat16)
    pad = jnp.zeros((HD - 4 * rows, 2 * HD), jnp.bfloat16)
    for step in range(2):
        biases = []
        for length, owner in zip(lengths, owners):
            bias = jnp.where(key < length, 0.0, NEG)
            biases.append(bias if step == 0 else jnp.where(owner, NEG, bias))
        extra_bias = jnp.where((lane % (2 * rows) < rows * (1 + step)) & (lane < 4 * rows), 0.0, NEG)
        stats = jnp.zeros((block, HD), jnp.float32)
        for side, refs in enumerate(((pack_ref, far_ref), (side_ref, cross_ref))):
            extras = []
            for index in range(2):
                pieces = []
                for ref in refs:
                    own = tail + (2 * step + index) * rows
                    clean = tail + (4 + index) * rows
                    pieces += [ref[own:own + rows, :], ref[clean:clean + rows, :]]
                extras.append(jnp.concatenate(pieces + [pad], axis=0))
            for half in range(2):
                head = (core ^ side) * 2 + half
                lanes = slice(half * HD, (half + 1) * HD)
                query = wide[pl.ds(step * 4 + head, block, stride=PARTS), :].astype(jnp.bfloat16)
                groups = [(ref[0:span, lanes], ref[span:2 * span, lanes], bias) for ref, bias in zip(refs, biases)]
                groups.append((extras[0][:, lanes], extras[1][:, lanes], extra_bias))
                scores = [
                    lax.dot_general(query, keys, NT, preferred_element_type=jnp.float32) + mask
                    for keys, _, mask in groups
                ]
                top = jnp.max(scores[0], axis=1, keepdims=True)
                for score in scores[1:]:
                    top = jnp.maximum(top, jnp.max(score, axis=1, keepdims=True))
                top = jnp.ceil(top)
                accum = jnp.zeros((block, 2 * HD), jnp.float32)
                for score, (_, values, _) in zip(scores, groups):
                    weights = jnp.exp2((score - top) * EXP2_SCALE).astype(jnp.bfloat16)
                    values = jnp.concatenate([values, ones[:values.shape[0]]], axis=1)
                    accum = accum + lax.dot_general(weights, values, NN, preferred_element_type=jnp.float32)
                wide_out[pl.ds(head * 2 + step, block, stride=BACK), :] = accum[:, :HD]
                total = accum[:, HD:]
                top = jnp.broadcast_to(top, (block, HD))
                top_hi = top.astype(jnp.bfloat16).astype(jnp.float32)
                total_hi = total.astype(jnp.bfloat16).astype(jnp.float32)
                for place, value in enumerate((top_hi, top - top_hi, total_hi, total - total_hi)):
                    stats = jnp.where(lane == 32 * place + head, value, stats)
        wide_out[pl.ds(8 + step, block, stride=BACK), :] = stats
    out_ref[...] = wide_out[...].astype(jnp.bfloat16)


def combine_kernel(recv_ref, out_ref, wide):
    chips = out_ref.shape[1] // (4 * HD)
    senders = recv_ref.shape[0] // BACK
    devices = senders // chips
    wide[...] = recv_ref[...].astype(jnp.float32)

    def rows_of(place):
        return wide[pl.ds(place, senders, stride=BACK), :].reshape(devices, chips, HD)

    for step in range(2):
        stats = rows_of(8 + step)
        for head in range(4):
            local = stats[:, :, head:head + 1] + stats[:, :, 32 + head:33 + head]
            total = stats[:, :, 64 + head:65 + head] + stats[:, :, 96 + head:97 + head]
            top = jnp.max(local, axis=0, keepdims=True)
            scale = jnp.exp2((local - top) * EXP2_SCALE)
            whole = jnp.sum(scale * total, axis=0)
            result = jnp.sum(scale * rows_of(head * 2 + step), axis=0) / whole
            for chip in range(chips):
                begin = (chip * 4 + head) * HD
                out_ref[step:step + 1, begin:begin + HD] = result[chip:chip + 1].astype(jnp.bfloat16)


def renew_kernel(evict_ref, near_ref, far_ref, cache_ref, new_ref):
    devices, _, rows, _ = near_ref.shape
    parity = lax.axis_index("cb")
    owner = lax.axis_index("ca") * 2 + parity == evict_ref[0]

    @pl.when(owner)
    def _():
        for ref, kind in ((near_ref, parity), (far_ref, 1 - parity)):
            for device in range(devices):
                place = pl.ds(pl.multiple_of((device * 2 + kind) * rows, rows), rows)
                for index in range(2):
                    new_ref[0, index, place, :] = ref[device, index]

    @pl.when(jnp.logical_not(owner))
    def _():
        new_ref[...] = cache_ref[...]


def call(kernel, out_shape, in_specs, scratch=(), name=None, limit=40, out=VMEM):
    several = isinstance(out_shape, tuple)
    return pl.pallas_call(
        kernel,
        out_shape=out_shape,
        in_specs=in_specs,
        out_specs=(out,) * len(out_shape) if several else out,
        scratch_shapes=list(scratch),
        compiler_params=pltpu.CompilerParams(vmem_limit_bytes=limit * 1024 * 1024),
        name=name,
    )


def body(queries, cache_kv, lengths, evict, own_kv, clean_kv):
    steps, _, features = queries.shape
    span, width = cache_kv.shape[2:]
    pairs = lax.axis_size("ca")
    chips = lax.axis_size("ha")
    rows = clean_kv.shape[1]
    tokens = pairs * chips
    bf16, f32 = jnp.bfloat16, jnp.float32
    shape = jax.ShapeDtypeStruct
    swap = [(0, 1), (1, 0)]
    pack = call(
        pack_kernel,
        shape((2 * span + 7 * rows, width), bf16),
        [SMEM] + [HBM] * 3,
        [pltpu.VMEM((rows, width), bf16), pltpu.SemaphoreType.DMA((9,))],
        name="pack",
        limit=60,
    )(lengths, cache_kv, own_kv, clean_kv)
    far = lax.ppermute(pack, "cb", swap)
    side = lax.ppermute(pack, "hb", swap)
    cross = lax.ppermute(far, "hb", swap)
    message, copies = call(
        spread_kernel,
        (shape((tokens * PARTS, HD), bf16), shape((pairs,) + clean_kv.shape, bf16)),
        [VMEM] * 2,
        [pltpu.VMEM((chips * PARTS, HD), f32)],
        name="spread",
    )(queries.reshape(steps, features), clean_kv)
    recv = lax.all_to_all(
        message.reshape(tokens, PARTS, HD), ("ca", "ha"), split_axis=0, concat_axis=0, tiled=True
    ).reshape(tokens * PARTS, HD)
    parts = call(
        attend_kernel,
        shape((tokens * BACK, HD), bf16),
        [SMEM] + [VMEM] * 5,
        [pltpu.VMEM((tokens * PARTS, HD), f32), pltpu.VMEM((tokens * BACK, HD), f32)],
        name="attend",
    )(evict, recv, pack, far, side, cross)
    _, copies = lax.optimization_barrier((recv, copies))
    near = lax.all_to_all(copies, "ca", split_axis=0, concat_axis=0, tiled=True)
    parts, near = lax.optimization_barrier((parts, near))
    back = lax.all_to_all(
        parts.reshape(tokens * BACK // 2, 2, HD), ("ca", "ha"), split_axis=0, concat_axis=0, tiled=True
    ).reshape(tokens * BACK, HD)
    attended = call(
        combine_kernel,
        shape((steps, features), bf16),
        [VMEM],
        [pltpu.VMEM((tokens * BACK, HD), f32)],
        name="combine",
    )(back)
    other = lax.ppermute(near, "cb", swap)
    new_cache = call(renew_kernel, shape(cache_kv.shape, bf16), [SMEM] + [VMEM] * 3, name="renew_cache")(
        evict, near, other, cache_kv
    )
    return (attended.reshape(steps, 1, features), new_cache)


def solution(mesh):
    ctx, heads = mesh.devices.shape
    split = jax.sharding.Mesh(mesh.devices.reshape(ctx // 2, 2, heads // 2, 2), ("ca", "cb", "ha", "hb"))
    ctx, heads = ("ca", "cb"), ("ha", "hb")
    in_specs = (
        P(None, ctx + heads, None),
        P(ctx, None, None, heads),
        P(ctx),
        P(),
        P(None, None, ctx, heads),
        P(None, ctx, heads),
    )
    out_specs = (P(None, ctx + heads, None), P(ctx, None, None, heads))
    return jax.shard_map(body, mesh=split, in_specs=in_specs, out_specs=out_specs, check_vma=False)
```

profile of v0, /device:TPU:6, one launch (start us, length us, event | category | flops | bytes accessed | tf_op | source)
XLA Modules:
  0.0 83.9 jit_solution(14857752749993512321)
XLA Ops:
  1.3 0.0 copy-start.2
  1.3 0.0 copy-start.3
  1.3 2.0 %pack.1.pack_ref = bf16[1136,256]{1,0:T(8,128)(2,1)} custom-call(s32[1]{0:T(128)S(6)} %copy.8.length_ref, bf16[1,2,512,256]{3,2,1,0:T(8,128)(2,1)} %cache_ref.3, bf16[2,2,16,256]{3,2,1,0:T(8,128)(2,1)} %own_ref.1, bf16[2,16,256]{2,1,0:T(8,128)(2,1)} %clean_ref.3), custom_call_target="tpu_custom_call" | custom-call | tf_op jit(solution)/shard_map/pack/pallas_call | solution.py:180
  3.3 0.0 copy-start
  3.3 4.4 %collective-permute-start = (bf16[1136,256]{1,0:T(8,128)(2,1)}, bf16[1136,256]{1,0:T(8,128)(2,1)S(1)}, u32[]{:S(2)}, u32[]{:S(2)}) collective-permute-start(bf16[1136,256]{1,0:T(8,128)(2,1)} %pack.1.pack_ref), channel_id=1, source_target_pairs={{0,16},{16,0},{1,17},{17,1},{2,18},{18,2},{3,19},{19,3},{4,20},{20... | collective-permute-start | bytes 1744904 | tf_op jit(solution)/shard_map/ppermute | solution.py:188
  7.7 0.0 copy-done.2
  7.7 0.0 copy-done.3
  7.7 0.8 spread.1
  8.5 18.9 %all-to-all-start = ((bf16[128,8,128]{2,1,0:T(8,128)(2,1)}), bf16[128,8,128]{2,1,0:T(8,128)(2,1)S(1)}, u32[]{:S(2)}, u32[]{:S(2)}) async-start(bf16[128,8,128]{2,1,0:T(8,128)(2,1)} %bitcast.1), calls=%async_computation | async-start | bytes 524288 | tf_op jit(solution)/shard_map/all_to_all | solution.py:198
  27.5 1.9 %collective-permute-start.1 = (bf16[1136,256]{1,0:T(8,128)(2,1)}, bf16[1136,256]{1,0:T(8,128)(2,1)S(1)}, u32[]{:S(2)}, u32[]{:S(2)}) collective-permute-start(bf16[1136,256]{1,0:T(8,128)(2,1)} %pack.1.pack_ref), channel_id=1, source_target_pairs={{0,1},{1,0},{2,3},{3,2},{4,5},{5,4},{6,7},{7,6},{8,9},{9,8},{10,11... | collective-permute-start | bytes 1744904 | tf_op jit(solution)/shard_map/ppermute | solution.py:189
  29.4 0.0 collective-permute-done.far_ref
  29.4 2.4 %collective-permute-start.2 = (bf16[1136,256]{1,0:T(8,128)(2,1)S(1)}, bf16[1136,256]{1,0:T(8,128)(2,1)S(1)}, u32[]{:S(2)}, u32[]{:S(2)}) collective-permute-start(bf16[1136,256]{1,0:T(8,128)(2,1)S(1)} %collective-permute-done.far_ref), channel_id=1, source_target_pairs={{0,1},{1,0},{2,3},{3,2},{4,5},{5,4},{6,7},{7,6},{8,9},{9,8},{10,11... | collective-permute-start | bytes 1744904 | tf_op jit(solution)/shard_map/ppermute | solution.py:190
  31.8 11.7 %all-to-all-done = bf16[128,8,128]{2,1,0:T(8,128)(2,1)S(1)} async-done(((bf16[128,8,128]{2,1,0:T(8,128)(2,1)}), bf16[128,8,128]{2,1,0:T(8,128)(2,1)S(1)}, u32[]{:S(2)}, u32[]{:S(2)}) %all-to-all-start) | async-done | bytes 262176 | tf_op jit(solution)/shard_map/all_to_all | solution.py:198
  43.5 3.5 %all-to-all-start.1 = ((bf16[16,2,16,256]{3,2,1,0:T(8,128)(2,1)}), bf16[16,2,16,256]{3,2,1,0:T(8,128)(2,1)S(1)}, u32[]{:S(2)}, u32[]{:S(2)}) async-start(bf16[16,2,16,256]{3,2,1,0:T(8,128)(2,1)} %get-tuple-element.9), calls=%async_computation.1 | async-start | bytes 524288 | tf_op jit(solution)/shard_map/all_to_all | solution.py:209
  47.7 0.0 collective-permute-done.1.side_ref
  47.7 0.0 collective-permute-done.2.cross_ref
  47.8 0.0 copy-done
  47.8 2.8 %attend.1 = bf16[1280,128]{1,0:T(8,128)(2,1)} custom-call(s32[1]{0:T(128)S(6)} %copy.9.evict_ref, bf16[1024,128]{1,0:T(8,128)(2,1)S(1)} %bitcast.7, bf16[1136,256]{1,0:T(8,128)(2,1)S(1)} %copy-done, bf16[1136,256]{1,0:T(8,128)(2,1)S(1)} %collective-permute-done.far_ref, bf16[1136,256]{1,0:T(8,128)(2,1)S(1)} %collective-permute-done.1.side_ref, ...), custom_call_target="tpu_custom_call" | custom-call | tf_op jit(solution)/shard_map/attend/pallas_call | solution.py:201
  50.6 0.0 copy-start.1
  50.6 8.2 %all-to-all-done.1.near_ref = bf16[16,2,16,256]{3,2,1,0:T(8,128)(2,1)S(1)} async-done(((bf16[16,2,16,256]{3,2,1,0:T(8,128)(2,1)}), bf16[16,2,16,256]{3,2,1,0:T(8,128)(2,1)S(1)}, u32[]{:S(2)}, u32[]{:S(2)}) %all-to-all-start.1) | async-done | bytes 262176 | tf_op jit(solution)/shard_map/all_to_all | solution.py:209
  58.8 8.0 %all-to-all-start.2 = ((bf16[640,2,128]{2,1,0:T(2,128)(2,1)}), bf16[640,2,128]{2,1,0:T(2,128)(2,1)S(1)}, u32[]{:S(2)}, u32[]{:S(2)}) async-start(bf16[640,2,128]{2,1,0:T(2,128)(2,1)} %bitcast.3), calls=%async_computation.2 | async-start | bytes 655360 | tf_op jit(solution)/shard_map/all_to_all | solution.py:211
  66.9 2.5 %collective-permute-start.3 = (bf16[16,2,16,256]{3,2,1,0:T(8,128)(2,1)S(1)}, bf16[16,2,16,256]{3,2,1,0:T(8,128)(2,1)S(1)}, u32[]{:S(2)}, u32[]{:S(2)}) collective-permute-start(bf16[16,2,16,256]{3,2,1,0:T(8,128)(2,1)S(1)} %all-to-all-done.1.near_ref), channel_id=1, source_target_pairs={{0,16},{16,0},{1,17},{17,1},{2,18},{18,2},{3,19},{19,3},{4,20},{20... | collective-permute-start | bytes 786440 | tf_op jit(solution)/shard_map/ppermute | solution.py:221
  69.3 10.2 %collective-permute-done.3.far_ref = bf16[16,2,16,256]{3,2,1,0:T(8,128)(2,1)S(1)} collective-permute-done((bf16[16,2,16,256]{3,2,1,0:T(8,128)(2,1)S(1)}, bf16[16,2,16,256]{3,2,1,0:T(8,128)(2,1)S(1)}, u32[]{:S(2)}, u32[]{:S(2)}) %collective-permute-start.3) | collective-permute-done | bytes 262176 | tf_op jit(solution)/shard_map/ppermute | solution.py:221
  79.6 0.0 copy-done.1
  79.6 0.8 renew_cache.1
  80.4 2.4 %all-to-all-done.2 = bf16[640,2,128]{2,1,0:T(2,128)(2,1)S(1)} async-done(((bf16[640,2,128]{2,1,0:T(2,128)(2,1)}), bf16[640,2,128]{2,1,0:T(2,128)(2,1)S(1)}, u32[]{:S(2)}, u32[]{:S(2)}) %all-to-all-start.2) | async-done | bytes 327712 | tf_op jit(solution)/shard_map/all_to_all | solution.py:211
  82.8 1.1 %combine.1 = bf16[2,4096]{1,0:T(2,128)(2,1)} custom-call(bf16[1280,128]{1,0:T(8,128)(2,1)S(1)} %bitcast.6), custom_call_target="tpu_custom_call" | custom-call | tf_op jit(solution)/shard_map/combine/pallas_call | solution.py:214
Async XLA Ops:
  1.3 6.4 %copy-start.2 = (bf16[2,16,256]{2,1,0:T(8,128)(2,1)S(1)}, bf16[2,16,256]{2,1,0:T(8,128)(2,1)}, u32[]{:S(2)}) copy-start(bf16[2,16,256]{2,1,0:T(8,128)(2,1)} %clean_ref.3) | copy-start | bytes 49156
  1.3 6.4 %copy-start.3 = (bf16[2,1,4096]{2,0,1:T(2,128)(2,1)S(1)}, bf16[2,1,4096]{2,0,1:T(2,128)(2,1)}, u32[]{:S(2)}) copy-start(bf16[2,1,4096]{2,0,1:T(2,128)(2,1)} %param.6) | copy-start | bytes 49156
  3.3 44.5 %copy-start = (bf16[1136,256]{1,0:T(8,128)(2,1)S(1)}, bf16[1136,256]{1,0:T(8,128)(2,1)}, u32[]{:S(2)}) copy-start(bf16[1136,256]{1,0:T(8,128)(2,1)} %pack.1.pack_ref) | copy-start | bytes 1744900
  3.3 26.2 %collective-permute-start = (bf16[1136,256]{1,0:T(8,128)(2,1)}, bf16[1136,256]{1,0:T(8,128)(2,1)S(1)}, u32[]{:S(2)}, u32[]{:S(2)}) collective-permute-start(bf16[1136,256]{1,0:T(8,128)(2,1)} %pack.1.pack_ref), channel_id=1, source_target_pairs={{0,16},{16,0},{1,17},{17,1},{2,18},{18,2},{3,19},{19,3},{4,20},{20... | collective-permute-start | bytes 1744904 | tf_op jit(solution)/shard_map/ppermute | solution.py:188
  8.5 35.0 %all-to-all-start = ((bf16[128,8,128]{2,1,0:T(8,128)(2,1)}), bf16[128,8,128]{2,1,0:T(8,128)(2,1)S(1)}, u32[]{:S(2)}, u32[]{:S(2)}) async-start(bf16[128,8,128]{2,1,0:T(8,128)(2,1)} %bitcast.1), calls=%async_computation | async-start | bytes 524288 | tf_op jit(solution)/shard_map/all_to_all | solution.py:198
  27.5 20.2 %collective-permute-start.1 = (bf16[1136,256]{1,0:T(8,128)(2,1)}, bf16[1136,256]{1,0:T(8,128)(2,1)S(1)}, u32[]{:S(2)}, u32[]{:S(2)}) collective-permute-start(bf16[1136,256]{1,0:T(8,128)(2,1)} %pack.1.pack_ref), channel_id=1, source_target_pairs={{0,1},{1,0},{2,3},{3,2},{4,5},{5,4},{6,7},{7,6},{8,9},{9,8},{10,11... | collective-permute-start | bytes 1744904 | tf_op jit(solution)/shard_map/ppermute | solution.py:189
  29.4 18.3 %collective-permute-start.2 = (bf16[1136,256]{1,0:T(8,128)(2,1)S(1)}, bf16[1136,256]{1,0:T(8,128)(2,1)S(1)}, u32[]{:S(2)}, u32[]{:S(2)}) collective-permute-start(bf16[1136,256]{1,0:T(8,128)(2,1)S(1)} %collective-permute-done.far_ref), channel_id=1, source_target_pairs={{0,1},{1,0},{2,3},{3,2},{4,5},{5,4},{6,7},{7,6},{8,9},{9,8},{10,11... | collective-permute-start | bytes 1744904 | tf_op jit(solution)/shard_map/ppermute | solution.py:190
  43.5 15.3 %all-to-all-start.1 = ((bf16[16,2,16,256]{3,2,1,0:T(8,128)(2,1)}), bf16[16,2,16,256]{3,2,1,0:T(8,128)(2,1)S(1)}, u32[]{:S(2)}, u32[]{:S(2)}) async-start(bf16[16,2,16,256]{3,2,1,0:T(8,128)(2,1)} %get-tuple-element.9), calls=%async_computation.1 | async-start | bytes 524288 | tf_op jit(solution)/shard_map/all_to_all | solution.py:209
  50.6 29.0 %copy-start.1 = (bf16[1,2,512,256]{3,2,1,0:T(8,128)(2,1)S(1)}, bf16[1,2,512,256]{3,2,1,0:T(8,128)(2,1)}, u32[]{:S(2)}) copy-start(bf16[1,2,512,256]{3,2,1,0:T(8,128)(2,1)} %cache_ref.3) | copy-start | bytes 1572868
  58.8 23.9 %all-to-all-start.2 = ((bf16[640,2,128]{2,1,0:T(2,128)(2,1)}), bf16[640,2,128]{2,1,0:T(2,128)(2,1)S(1)}, u32[]{:S(2)}, u32[]{:S(2)}) async-start(bf16[640,2,128]{2,1,0:T(2,128)(2,1)} %bitcast.3), calls=%async_computation.2 | async-start | bytes 655360 | tf_op jit(solution)/shard_map/all_to_all | solution.py:211
  66.9 12.7 %collective-permute-start.3 = (bf16[16,2,16,256]{3,2,1,0:T(8,128)(2,1)S(1)}, bf16[16,2,16,256]{3,2,1,0:T(8,128)(2,1)S(1)}, u32[]{:S(2)}, u32[]{:S(2)}) collective-permute-start(bf16[16,2,16,256]{3,2,1,0:T(8,128)(2,1)S(1)} %all-to-all-done.1.near_ref), channel_id=1, source_target_pairs={{0,16},{16,0},{1,17},{17,1},{2,18},{18,2},{3,19},{19,3},{4,20},{20... | collective-permute-start | bytes 786440 | tf_op jit(solution)/shard_map/ppermute | solution.py:221
where the time goes:
time: 84.3 us; the launch traced here: 83.9 us
  starting transfers between devices  41.7 us (49%)
  waiting for transfers between devices  32.5 us (39%)
  Pallas kernels  7.55 us (9%)
  between operations  2.06 us (2%)
    all_to_all x1, starting transfers between devices, body(): lax.all_to_all(message.reshape(tokens, PARTS, HD), ('ca', 'ha'), split_ax...  18.9 us
    all_to_all x1, waiting for transfers between devices, body(): lax.all_to_all(message.reshape(tokens, PARTS, HD), ('ca', 'ha'), split_ax...  11.7 us
    ppermute x1, waiting for transfers between devices, body(): other = lax.ppermute(near, 'cb', swap)  10.2 us
    all_to_all x1, waiting for transfers between devices, body(): near = lax.all_to_all(copies, 'ca', split_axis=0, concat_axis=0, tiled=True)  8.2 us
    all_to_all x1, starting transfers between devices, body(): lax.all_to_all(parts.reshape(tokens * BACK // 2, 2, HD), ('ca', 'ha'), sp...  8.04 us
    ppermute x1, starting transfers between devices, body(): far = lax.ppermute(pack, 'cb', swap)  4.41 us
    all_to_all x1, starting transfers between devices, body(): near = lax.all_to_all(copies, 'ca', split_axis=0, concat_axis=0, tiled=True)  3.53 us
    pallas_call x1, Pallas kernels, body(): call(attend_kernel, shape((tokens * BACK, HD), bf16), [SMEM] + [VMEM] * 5...  2.84 us
  transfers between devices with their start and end apart: 7, of which 4 were waited for; matrix products, arithmetic and copies ran while one was open for 0% of the time, Pallas kernels for 5%

commit v1 on v0

--- a/solution.py
+++ b/solution.py
@@ -21,10 +21,9 @@
 
 def spread_kernel(q_ref, clean_ref, out_ref, copies_ref, rows):
     count = rows.shape[0]
-    for row in range(count):
-        chip, step, head = row // PARTS, row // 4 % 2, row % 4
-        start = (chip * 4 + head) * HD
-        rows[row:row + 1, :] = q_ref[step:step + 1, start:start + HD].astype(jnp.float32)
+    for head in range(count // 2):
+        piece = q_ref[:, head * HD:(head + 1) * HD].astype(jnp.float32)
+        rows[pl.ds(head // 4 * PARTS + head % 4, 2, stride=4), :] = piece
     message = rows[...].astype(out_ref.dtype)
     for dest in range(out_ref.shape[0] // count):
         out_ref[dest * count:(dest + 1) * count, :] = message
@@ -120,17 +119,18 @@
     wide[...] = recv_ref[...].astype(jnp.float32)
 
     def rows_of(place):
-        return wide[pl.ds(place, senders, stride=BACK), :].reshape(devices, chips, HD)
+        return wide[pl.ds(place, senders, stride=BACK), :]
 
     for step in range(2):
         stats = rows_of(8 + step)
+        local = (stats + pltpu.roll(stats, HD - 32, axis=1)).reshape(devices, chips, HD)
+        total = (pltpu.roll(stats, HD - 64, axis=1) + pltpu.roll(stats, HD - 96, axis=1)).reshape(devices, chips, HD)
+        top = jnp.max(local, axis=0, keepdims=True)
+        scale = jnp.exp2((local - top) * EXP2_SCALE)
+        scale = scale / jnp.sum(scale * total, axis=0, keepdims=True)
         for head in range(4):
-            local = stats[:, :, head:head + 1] + stats[:, :, 32 + head:33 + head]
-            total = stats[:, :, 64 + head:65 + head] + stats[:, :, 96 + head:97 + head]
-            top = jnp.max(local, axis=0, keepdims=True)
-            scale = jnp.exp2((local - top) * EXP2_SCALE)
-            whole = jnp.sum(scale * total, axis=0)
-            result = jnp.sum(scale * rows_of(head * 2 + step), axis=0) / whole
+            accum = rows_of(head * 2 + step).reshape(devices, chips, HD)
+            result = jnp.sum(scale[:, :, head:head + 1] * accum, axis=0)
             for chip in range(chips):
                 begin = (chip * 4 + head) * HD
                 out_ref[step:step + 1, begin:begin + HD] = result[chip:chip + 1].astype(jnp.bfloat16)

time: 84.3 us -> 84.3 us (level)
  no operation moved by 1% of the time
where the time goes in v1:
time: 84.3 us; the launch traced here: 83.9 us
  starting transfers between devices  41.7 us (49%)
  waiting for transfers between devices  32.5 us (39%)
  Pallas kernels  7.56 us (9%)
  between operations  2.06 us (2%)
    all_to_all x1, starting transfers between devices, body(): lax.all_to_all(message.reshape(tokens, PARTS, HD), ('ca', 'ha'), split_ax...  18.9 us
    all_to_all x1, waiting for transfers between devices, body(): lax.all_to_all(message.reshape(tokens, PARTS, HD), ('ca', 'ha'), split_ax...  11.7 us
    ppermute x1, waiting for transfers between devices, body(): other = lax.ppermute(near, 'cb', swap)  10.2 us
    all_to_all x1, waiting for transfers between devices, body(): near = lax.all_to_all(copies, 'ca', split_axis=0, concat_axis=0, tiled=True)  8.2 us
    all_to_all x1, starting transfers between devices, body(): lax.all_to_all(parts.reshape(tokens * BACK // 2, 2, HD), ('ca', 'ha'), sp...  8.04 us
    ppermute x1, starting transfers between devices, body(): far = lax.ppermute(pack, 'cb', swap)  4.41 us
    all_to_all x1, starting transfers between devices, body(): near = lax.all_to_all(copies, 'ca', split_axis=0, concat_axis=0, tiled=True)  3.53 us
    pallas_call x1, Pallas kernels, body(): call(attend_kernel, shape((tokens * BACK, HD), bf16), [SMEM] + [VMEM] * 5...  2.84 us
  transfers between devices with their start and end apart: 7, of which 4 were waited for; matrix products, arithmetic and copies ran while one was open for 0% of the time, Pallas kernels for 5%

profile of v1, /device:TPU:6, one launch (start us, length us, event | category | flops | bytes accessed | tf_op | source)
XLA Modules:
  0.0 83.9 jit_solution(18400074607933926943)
XLA Ops:
  1.3 0.0 copy-start.2
  1.3 0.0 copy-start.3
  1.3 2.0 %pack.1.pack_ref = bf16[1136,256]{1,0:T(8,128)(2,1)} custom-call(s32[1]{0:T(128)S(6)} %copy.8.length_ref, bf16[1,2,512,256]{3,2,1,0:T(8,128)(2,1)} %cache_ref.3, bf16[2,2,16,256]{3,2,1,0:T(8,128)(2,1)} %own_ref.1, bf16[2,16,256]{2,1,0:T(8,128)(2,1)} %clean_ref.3), custom_call_target="tpu_custom_call" | custom-call | tf_op jit(solution)/shard_map/pack/pallas_call | solution.py:180
  3.3 0.0 copy-start
  3.3 4.4 %collective-permute-start = (bf16[1136,256]{1,0:T(8,128)(2,1)}, bf16[1136,256]{1,0:T(8,128)(2,1)S(1)}, u32[]{:S(2)}, u32[]{:S(2)}) collective-permute-start(bf16[1136,256]{1,0:T(8,128)(2,1)} %pack.1.pack_ref), channel_id=1, source_target_pairs={{0,16},{16,0},{1,17},{17,1},{2,18},{18,2},{3,19},{19,3},{4,20},{20... | collective-permute-start | bytes 1744904 | tf_op jit(solution)/shard_map/ppermute | solution.py:188
  7.7 0.0 copy-done.2
  7.7 0.0 copy-done.3
  7.7 0.8 spread.1
  8.5 18.9 %all-to-all-start = ((bf16[128,8,128]{2,1,0:T(8,128)(2,1)}), bf16[128,8,128]{2,1,0:T(8,128)(2,1)S(1)}, u32[]{:S(2)}, u32[]{:S(2)}) async-start(bf16[128,8,128]{2,1,0:T(8,128)(2,1)} %bitcast.1), calls=%async_computation | async-start | bytes 524288 | tf_op jit(solution)/shard_map/all_to_all | solution.py:198
  27.5 1.9 %collective-permute-start.1 = (bf16[1136,256]{1,0:T(8,128)(2,1)}, bf16[1136,256]{1,0:T(8,128)(2,1)S(1)}, u32[]{:S(2)}, u32[]{:S(2)}) collective-permute-start(bf16[1136,256]{1,0:T(8,128)(2,1)} %pack.1.pack_ref), channel_id=1, source_target_pairs={{0,1},{1,0},{2,3},{3,2},{4,5},{5,4},{6,7},{7,6},{8,9},{9,8},{10,11... | collective-permute-start | bytes 1744904 | tf_op jit(solution)/shard_map/ppermute | solution.py:189
  29.4 0.0 collective-permute-done.far_ref
  29.4 2.4 %collective-permute-start.2 = (bf16[1136,256]{1,0:T(8,128)(2,1)S(1)}, bf16[1136,256]{1,0:T(8,128)(2,1)S(1)}, u32[]{:S(2)}, u32[]{:S(2)}) collective-permute-start(bf16[1136,256]{1,0:T(8,128)(2,1)S(1)} %collective-permute-done.far_ref), channel_id=1, source_target_pairs={{0,1},{1,0},{2,3},{3,2},{4,5},{5,4},{6,7},{7,6},{8,9},{9,8},{10,11... | collective-permute-start | bytes 1744904 | tf_op jit(solution)/shard_map/ppermute | solution.py:190
  31.8 11.7 %all-to-all-done = bf16[128,8,128]{2,1,0:T(8,128)(2,1)S(1)} async-done(((bf16[128,8,128]{2,1,0:T(8,128)(2,1)}), bf16[128,8,128]{2,1,0:T(8,128)(2,1)S(1)}, u32[]{:S(2)}, u32[]{:S(2)}) %all-to-all-start) | async-done | bytes 262176 | tf_op jit(solution)/shard_map/all_to_all | solution.py:198
  43.5 3.5 %all-to-all-start.1 = ((bf16[16,2,16,256]{3,2,1,0:T(8,128)(2,1)}), bf16[16,2,16,256]{3,2,1,0:T(8,128)(2,1)S(1)}, u32[]{:S(2)}, u32[]{:S(2)}) async-start(bf16[16,2,16,256]{3,2,1,0:T(8,128)(2,1)} %get-tuple-element.9), calls=%async_computation.1 | async-start | bytes 524288 | tf_op jit(solution)/shard_map/all_to_all | solution.py:209
  47.7 0.0 collective-permute-done.1.side_ref
  47.7 0.0 collective-permute-done.2.cross_ref
  47.8 0.0 copy-done
  47.8 2.8 %attend.1 = bf16[1280,128]{1,0:T(8,128)(2,1)} custom-call(s32[1]{0:T(128)S(6)} %copy.9.evict_ref, bf16[1024,128]{1,0:T(8,128)(2,1)S(1)} %bitcast.7, bf16[1136,256]{1,0:T(8,128)(2,1)S(1)} %copy-done, bf16[1136,256]{1,0:T(8,128)(2,1)S(1)} %collective-permute-done.far_ref, bf16[1136,256]{1,0:T(8,128)(2,1)S(1)} %collective-permute-done.1.side_ref, ...), custom_call_target="tpu_custom_call" | custom-call | tf_op jit(solution)/shard_map/attend/pallas_call | solution.py:201
  50.6 0.0 copy-start.1
  50.6 8.2 %all-to-all-done.1.near_ref = bf16[16,2,16,256]{3,2,1,0:T(8,128)(2,1)S(1)} async-done(((bf16[16,2,16,256]{3,2,1,0:T(8,128)(2,1)}), bf16[16,2,16,256]{3,2,1,0:T(8,128)(2,1)S(1)}, u32[]{:S(2)}, u32[]{:S(2)}) %all-to-all-start.1) | async-done | bytes 262176 | tf_op jit(solution)/shard_map/all_to_all | solution.py:209
  58.8 8.0 %all-to-all-start.2 = ((bf16[640,2,128]{2,1,0:T(2,128)(2,1)}), bf16[640,2,128]{2,1,0:T(2,128)(2,1)S(1)}, u32[]{:S(2)}, u32[]{:S(2)}) async-start(bf16[640,2,128]{2,1,0:T(2,128)(2,1)} %bitcast.3), calls=%async_computation.2 | async-start | bytes 655360 | tf_op jit(solution)/shard_map/all_to_all | solution.py:211
  66.9 2.5 %collective-permute-start.3 = (bf16[16,2,16,256]{3,2,1,0:T(8,128)(2,1)S(1)}, bf16[16,2,16,256]{3,2,1,0:T(8,128)(2,1)S(1)}, u32[]{:S(2)}, u32[]{:S(2)}) collective-permute-start(bf16[16,2,16,256]{3,2,1,0:T(8,128)(2,1)S(1)} %all-to-all-done.1.near_ref), channel_id=1, source_target_pairs={{0,16},{16,0},{1,17},{17,1},{2,18},{18,2},{3,19},{19,3},{4,20},{20... | collective-permute-start | bytes 786440 | tf_op jit(solution)/shard_map/ppermute | solution.py:221
  69.3 10.2 %collective-permute-done.3.far_ref = bf16[16,2,16,256]{3,2,1,0:T(8,128)(2,1)S(1)} collective-permute-done((bf16[16,2,16,256]{3,2,1,0:T(8,128)(2,1)S(1)}, bf16[16,2,16,256]{3,2,1,0:T(8,128)(2,1)S(1)}, u32[]{:S(2)}, u32[]{:S(2)}) %collective-permute-start.3) | collective-permute-done | bytes 262176 | tf_op jit(solution)/shard_map/ppermute | solution.py:221
  79.6 0.0 copy-done.1
  79.6 0.8 renew_cache.1
  80.4 2.4 %all-to-all-done.2 = bf16[640,2,128]{2,1,0:T(2,128)(2,1)S(1)} async-done(((bf16[640,2,128]{2,1,0:T(2,128)(2,1)}), bf16[640,2,128]{2,1,0:T(2,128)(2,1)S(1)}, u32[]{:S(2)}, u32[]{:S(2)}) %all-to-all-start.2) | async-done | bytes 327712 | tf_op jit(solution)/shard_map/all_to_all | solution.py:211
  82.8 1.1 %combine.1 = bf16[2,4096]{1,0:T(2,128)(2,1)} custom-call(bf16[1280,128]{1,0:T(8,128)(2,1)S(1)} %bitcast.6), custom_call_target="tpu_custom_call" | custom-call | tf_op jit(solution)/shard_map/combine/pallas_call | solution.py:214
Async XLA Ops:
  1.3 6.4 %copy-start.2 = (bf16[2,16,256]{2,1,0:T(8,128)(2,1)S(1)}, bf16[2,16,256]{2,1,0:T(8,128)(2,1)}, u32[]{:S(2)}) copy-start(bf16[2,16,256]{2,1,0:T(8,128)(2,1)} %clean_ref.3) | copy-start | bytes 49156
  1.3 6.4 %copy-start.3 = (bf16[2,1,4096]{2,0,1:T(2,128)(2,1)S(1)}, bf16[2,1,4096]{2,0,1:T(2,128)(2,1)}, u32[]{:S(2)}) copy-start(bf16[2,1,4096]{2,0,1:T(2,128)(2,1)} %param.6) | copy-start | bytes 49156
  3.3 44.5 %copy-start = (bf16[1136,256]{1,0:T(8,128)(2,1)S(1)}, bf16[1136,256]{1,0:T(8,128)(2,1)}, u32[]{:S(2)}) copy-start(bf16[1136,256]{1,0:T(8,128)(2,1)} %pack.1.pack_ref) | copy-start | bytes 1744900
  3.3 26.2 %collective-permute-start = (bf16[1136,256]{1,0:T(8,128)(2,1)}, bf16[1136,256]{1,0:T(8,128)(2,1)S(1)}, u32[]{:S(2)}, u32[]{:S(2)}) collective-permute-start(bf16[1136,256]{1,0:T(8,128)(2,1)} %pack.1.pack_ref), channel_id=1, source_target_pairs={{0,16},{16,0},{1,17},{17,1},{2,18},{18,2},{3,19},{19,3},{4,20},{20... | collective-permute-start | bytes 1744904 | tf_op jit(solution)/shard_map/ppermute | solution.py:188
  8.5 35.0 %all-to-all-start = ((bf16[128,8,128]{2,1,0:T(8,128)(2,1)}), bf16[128,8,128]{2,1,0:T(8,128)(2,1)S(1)}, u32[]{:S(2)}, u32[]{:S(2)}) async-start(bf16[128,8,128]{2,1,0:T(8,128)(2,1)} %bitcast.1), calls=%async_computation | async-start | bytes 524288 | tf_op jit(solution)/shard_map/all_to_all | solution.py:198
  27.5 20.2 %collective-permute-start.1 = (bf16[1136,256]{1,0:T(8,128)(2,1)}, bf16[1136,256]{1,0:T(8,128)(2,1)S(1)}, u32[]{:S(2)}, u32[]{:S(2)}) collective-permute-start(bf16[1136,256]{1,0:T(8,128)(2,1)} %pack.1.pack_ref), channel_id=1, source_target_pairs={{0,1},{1,0},{2,3},{3,2},{4,5},{5,4},{6,7},{7,6},{8,9},{9,8},{10,11... | collective-permute-start | bytes 1744904 | tf_op jit(solution)/shard_map/ppermute | solution.py:189
  29.4 18.3 %collective-permute-start.2 = (bf16[1136,256]{1,0:T(8,128)(2,1)S(1)}, bf16[1136,256]{1,0:T(8,128)(2,1)S(1)}, u32[]{:S(2)}, u32[]{:S(2)}) collective-permute-start(bf16[1136,256]{1,0:T(8,128)(2,1)S(1)} %collective-permute-done.far_ref), channel_id=1, source_target_pairs={{0,1},{1,0},{2,3},{3,2},{4,5},{5,4},{6,7},{7,6},{8,9},{9,8},{10,11... | collective-permute-start | bytes 1744904 | tf_op jit(solution)/shard_map/ppermute | solution.py:190
  43.5 15.3 %all-to-all-start.1 = ((bf16[16,2,16,256]{3,2,1,0:T(8,128)(2,1)}), bf16[16,2,16,256]{3,2,1,0:T(8,128)(2,1)S(1)}, u32[]{:S(2)}, u32[]{:S(2)}) async-start(bf16[16,2,16,256]{3,2,1,0:T(8,128)(2,1)} %get-tuple-element.9), calls=%async_computation.1 | async-start | bytes 524288 | tf_op jit(solution)/shard_map/all_to_all | solution.py:209
  50.6 29.0 %copy-start.1 = (bf16[1,2,512,256]{3,2,1,0:T(8,128)(2,1)S(1)}, bf16[1,2,512,256]{3,2,1,0:T(8,128)(2,1)}, u32[]{:S(2)}) copy-start(bf16[1,2,512,256]{3,2,1,0:T(8,128)(2,1)} %cache_ref.3) | copy-start | bytes 1572868
  58.8 23.9 %all-to-all-start.2 = ((bf16[640,2,128]{2,1,0:T(2,128)(2,1)}), bf16[640,2,128]{2,1,0:T(2,128)(2,1)S(1)}, u32[]{:S(2)}, u32[]{:S(2)}) async-start(bf16[640,2,128]{2,1,0:T(2,128)(2,1)} %bitcast.3), calls=%async_computation.2 | async-start | bytes 655360 | tf_op jit(solution)/shard_map/all_to_all | solution.py:211
  66.9 12.7 %collective-permute-start.3 = (bf16[16,2,16,256]{3,2,1,0:T(8,128)(2,1)S(1)}, bf16[16,2,16,256]{3,2,1,0:T(8,128)(2,1)S(1)}, u32[]{:S(2)}, u32[]{:S(2)}) collective-permute-start(bf16[16,2,16,256]{3,2,1,0:T(8,128)(2,1)S(1)} %all-to-all-done.1.near_ref), channel_id=1, source_target_pairs={{0,16},{16,0},{1,17},{17,1},{2,18},{18,2},{3,19},{19,3},{4,20},{20... | collective-permute-start | bytes 786440 | tf_op jit(solution)/shard_map/ppermute | solution.py:221

commit v2 on v0

--- a/solution.py
+++ b/solution.py
@@ -31,30 +31,31 @@
         copies_ref[dest] = clean_ref[...]
 
 
-def pack_kernel(length_ref, cache_ref, own_ref, clean_ref, pack_ref, digit_rows, sems):
+def pack_kernel(length_ref, cache_ref, own_ref, clean_ref, keys_ref, values_ref, sems):
     span, rows = cache_ref.shape[2], clean_ref.shape[1]
-    pieces = [(cache_ref.at[0, index], span) for index in range(2)]
-    pieces += [(own_ref.at[step, index], rows) for step in range(2) for index in range(2)]
-    pieces += [(clean_ref.at[index], rows) for index in range(2)]
-    pieces += [(digit_rows, rows)]
     length = length_ref[0]
     lane = lax.broadcasted_iota(jnp.int32, (rows, 2 * HD), 1)
-    digits = jnp.where(lane < HD, length // 8, length % 8)
-    digit_rows[...] = digits.astype(jnp.float32).astype(digit_rows.dtype)
-    place, copies = 0, []
-    for number, (piece, count) in enumerate(pieces):
-        copies.append(pltpu.make_async_copy(piece, pack_ref.at[pl.ds(place, count)], sems.at[number]))
-        copies[-1].start()
-        place += count
+    digits = jnp.where(lane < HD, length // 8, length % 8).astype(jnp.float32)
+    copies = []
+    for index, out_ref in enumerate((keys_ref, values_ref)):
+        pieces = ((cache_ref.at[0, index], span), (own_ref.at[0, index], rows))
+        pieces += ((own_ref.at[1, index], rows), (clean_ref.at[index], rows))
+        place = 0
+        for piece, count in pieces:
+            copies.append(pltpu.make_async_copy(piece, out_ref.at[pl.ds(place, count)], sems.at[len(copies)]))
+            copies[-1].start()
+            place += count
+        out_ref[place:place + rows, :] = digits.astype(out_ref.dtype)
     for copy in copies:
         copy.wait()
 
 
-def attend_kernel(evict_ref, recv_ref, pack_ref, far_ref, side_ref, cross_ref, out_ref, wide, wide_out):
+def attend_kernel(evict_ref, recv_ref, *refs):
+    *packs, out_ref, wide, wide_out = refs
+    pack, far, side_pack, cross = packs[0:2], packs[2:4], packs[4:6], packs[6:8]
     block = recv_ref.shape[0] // PARTS
     rows = 16
-    span = (pack_ref.shape[0] - 7 * rows) // 2
-    tail = 2 * span
+    span = pack[0].shape[0] - 4 * rows
     me = lax.axis_index("ca") * 2 + lax.axis_index("cb")
     core = lax.axis_index("hb")
     owners = [me == evict_ref[0], (me ^ 1) == evict_ref[0]]
@@ -62,8 +63,8 @@
     key = lax.broadcasted_iota(jnp.int32, (1, span), 1).astype(jnp.float32)
     lane = lax.broadcasted_iota(jnp.int32, (1, HD), 1)
     lengths = []
-    for ref in (pack_ref, far_ref):
-        digits = ref[tail + 6 * rows:tail + 7 * rows, :].astype(jnp.float32)[0:1]
+    for ref in (pack[0], far[0]):
+        digits = ref[span + 3 * rows:span + 4 * rows, :].astype(jnp.float32)[0:1]
         lengths.append(jnp.concatenate([digits[:, :HD] * 8.0 + digits[:, HD:]] * (span // HD), axis=1))
     ones = jnp.ones((span, HD), jnp.bfloat16)
     pad = jnp.zeros((HD - 4 * rows, 2 * HD), jnp.bfloat16)
@@ -74,20 +75,20 @@
             biases.append(bias if step == 0 else jnp.where(owner, NEG, bias))
         extra_bias = jnp.where((lane % (2 * rows) < rows * (1 + step)) & (lane < 4 * rows), 0.0, NEG)
         stats = jnp.zeros((block, HD), jnp.float32)
-        for side, refs in enumerate(((pack_ref, far_ref), (side_ref, cross_ref))):
+        for side, pairs in enumerate(((pack, far), (side_pack, cross))):
             extras = []
             for index in range(2):
                 pieces = []
-                for ref in refs:
-                    own = tail + (2 * step + index) * rows
-                    clean = tail + (4 + index) * rows
-                    pieces += [ref[own:own + rows, :], ref[clean:clean + rows, :]]
+                for pair in pairs:
+                    own = span + step * rows
+                    clean = span + 2 * rows
+                    pieces += [pair[index][own:own + rows, :], pair[index][clean:clean + rows, :]]
                 extras.append(jnp.concatenate(pieces + [pad], axis=0))
             for half in range(2):
                 head = (core ^ side) * 2 + half
                 lanes = slice(half * HD, (half + 1) * HD)
                 query = wide[pl.ds(step * 4 + head, block, stride=PARTS), :].astype(jnp.bfloat16)
-                groups = [(ref[0:span, lanes], ref[span:2 * span, lanes], bias) for ref, bias in zip(refs, biases)]
+                groups = [(pair[0][0:span, lanes], pair[1][0:span, lanes], bias) for pair, bias in zip(pairs, biases)]
                 groups.append((extras[0][:, lanes], extras[1][:, lanes], extra_bias))
                 scores = [
                     lax.dot_general(query, keys, NT, preferred_element_type=jnp.float32) + mask
@@ -179,15 +180,15 @@
     swap = [(0, 1), (1, 0)]
     pack = call(
         pack_kernel,
-        shape((2 * span + 7 * rows, width), bf16),
+        (shape((span + 4 * rows, width), bf16),) * 2,
         [SMEM] + [HBM] * 3,
-        [pltpu.VMEM((rows, width), bf16), pltpu.SemaphoreType.DMA((9,))],
+        [pltpu.SemaphoreType.DMA((8,))],
         name="pack",
         limit=60,
     )(lengths, cache_kv, own_kv, clean_kv)
-    far = lax.ppermute(pack, "cb", swap)
-    side = lax.ppermute(pack, "hb", swap)
-    cross = lax.ppermute(far, "hb", swap)
+    far = [lax.ppermute(array, "cb", swap) for array in pack]
+    side = [lax.ppermute(array, "hb", swap) for array in pack]
+    cross = [lax.ppermute(array, "hb", swap) for array in far]
     message, copies = call(
         spread_kernel,
         (shape((tokens * PARTS, HD), bf16), shape((pairs,) + clean_kv.shape, bf16)),
@@ -201,10 +202,10 @@
     parts = call(
         attend_kernel,
         shape((tokens * BACK, HD), bf16),
-        [SMEM] + [VMEM] * 5,
+        [SMEM] + [VMEM] * 9,
         [pltpu.VMEM((tokens * PARTS, HD), f32), pltpu.VMEM((tokens * BACK, HD), f32)],
         name="attend",
-    )(evict, recv, pack, far, side, cross)
+    )(evict, recv, *pack, *far, *side, *cross)
     _, copies = lax.optimization_barrier((recv, copies))
     near = lax.all_to_all(copies, "ca", split_axis=0, concat_axis=0, tiled=True)
     parts, near = lax.optimization_barrier((parts, near))

time: 84.3 us -> 89.5 us (1.062)
  starting transfers between devices: 41.7 us -> 54.4 us
  waiting for transfers between devices: 32.5 us -> 22.4 us
  local copies, waits for them, and re-layouts: 0.02 us -> 2.4 us
    all_to_all x1, waiting for transfers between devices: 8.2 us -> 0.01 us  [body(): near = lax.all_to_all(copies, 'ca', split_axis=0, concat_axis=0, tiled=True)]
    ppermute x3 -> x6, starting transfers between devices: 8.74 us -> 14.6 us  [the longest x2 5.97 us: body(): far = [lax.ppermute(array, 'cb', swap) for array in pack]]
    all_to_all x1, starting transfers between devices: 8.04 us -> 13 us  [body(): lax.all_to_all(parts.reshape(tokens * BACK // 2, 2, HD), ('ca', 'ha'), sp...]
    all_to_all x1, waiting for transfers between devices: 11.7 us -> 7.72 us  [body(): lax.all_to_all(message.reshape(tokens, PARTS, HD), ('ca', 'ha'), split_ax...]
    unnamed x8 -> x10, local copies, waits for them, and re-layouts: 0.02 us -> 2.4 us
    ppermute x1, waiting for transfers between devices: 10.2 us -> 12.4 us  [body(): other = lax.ppermute(near, 'cb', swap)]
    ppermute x1, starting transfers between devices: 2.48 us -> 3.38 us  [body(): other = lax.ppermute(near, 'cb', swap)]
    all_to_all x1, starting transfers between devices: 18.9 us -> 19.8 us  [body(): lax.all_to_all(message.reshape(tokens, PARTS, HD), ('ca', 'ha'), split_ax...]
  transfers between devices with their start and end apart: 7 -> 10, of which waited for: 4 -> 4; matrix products, arithmetic and copies ran while one was open for 0% -> 0% of each run, Pallas kernels for 5% -> 6%
where the time goes in v2:
time: 89.5 us; the launch traced here: 88.8 us
  starting transfers between devices  54.4 us (61%)
  waiting for transfers between devices  22.4 us (25%)
  Pallas kernels  7.5 us (8%)
  local copies, waits for them, and re-layouts  2.4 us (3%)
  between operations  2.08 us (2%)
    all_to_all x1, starting transfers between devices, body(): lax.all_to_all(message.reshape(tokens, PARTS, HD), ('ca', 'ha'), split_ax...  19.8 us
    all_to_all x1, starting transfers between devices, body(): lax.all_to_all(parts.reshape(tokens * BACK // 2, 2, HD), ('ca', 'ha'), sp...  13 us
    ppermute x1, waiting for transfers between devices, body(): other = lax.ppermute(near, 'cb', swap)  12.4 us
    all_to_all x1, waiting for transfers between devices, body(): lax.all_to_all(message.reshape(tokens, PARTS, HD), ('ca', 'ha'), split_ax...  7.72 us
    ppermute x2, starting transfers between devices, body(): far = [lax.ppermute(array, 'cb', swap) for array in pack]  5.97 us
    ppermute x2, starting transfers between devices, body(): cross = [lax.ppermute(array, 'hb', swap) for array in far]  4.33 us
    ppermute x2, starting transfers between devices, body(): side = [lax.ppermute(array, 'hb', swap) for array in pack]  4.33 us
    all_to_all x1, starting transfers between devices, body(): near = lax.all_to_all(copies, 'ca', split_axis=0, concat_axis=0, tiled=True)  3.53 us
  transfers between devices with their start and end apart: 10, of which 4 were waited for; matrix products, arithmetic and copies ran while one was open for 0% of the time, Pallas kernels for 6%

profile of v2, /device:TPU:6, one launch (start us, length us, event | category | flops | bytes accessed | tf_op | source)
XLA Modules:
  0.0 88.8 jit_solution(9740106463266540558)
XLA Ops:
  0.6 0.0 copy-start.3
  0.6 0.7 copy-done.3
  1.4 0.7 copy-done.4
  2.1 0.8 spread.1
  2.9 19.8 %all-to-all-start = ((bf16[128,8,128]{2,1,0:T(8,128)(2,1)}), bf16[128,8,128]{2,1,0:T(8,128)(2,1)S(1)}, u32[]{:S(2)}, u32[]{:S(2)}) async-start(bf16[128,8,128]{2,1,0:T(8,128)(2,1)} %bitcast.1), calls=%async_computation | async-start | bytes 524288 | tf_op jit(solution)/shard_map/all_to_all | solution.py:199
  23.4 2.0 %pack.1 = (bf16[576,256]{1,0:T(8,128)(2,1)}, bf16[576,256]{1,0:T(8,128)(2,1)}) custom-call(s32[1]{0:T(128)S(6)} %copy.8.length_ref, bf16[1,2,512,256]{3,2,1,0:T(8,128)(2,1)} %cache_ref.3, bf16[2,2,16,256]{3,2,1,0:T(8,128)(2,1)} %own_ref.1, bf16[2,16,256]{2,1,0:T(8,128)(2,1)} %clean_ref.3), custom_call_target="tpu_custom_call" | custom-call | tf_op jit(solution)/shard_map/pack/pallas_call | solution.py:181
  25.4 0.0 copy-start.1
  25.4 3.5 %collective-permute-start = (bf16[576,256]{1,0:T(8,128)(2,1)}, bf16[576,256]{1,0:T(8,128)(2,1)S(1)}, u32[]{:S(2)}, u32[]{:S(2)}) collective-permute-start(bf16[576,256]{1,0:T(8,128)(2,1)} %get-tuple-element.10.refs_0_), channel_id=1, source_target_pairs={{0,16},{16,0},{1,17},{17,1},{2,18},{18,2},{3,19},{19,3},{4,20},{20... | collective-permute-start | bytes 884744 | tf_op jit(solution)/shard_map/ppermute | solution.py:189
  28.9 2.5 %collective-permute-start.1 = (bf16[576,256]{1,0:T(8,128)(2,1)}, bf16[576,256]{1,0:T(8,128)(2,1)S(1)}, u32[]{:S(2)}, u32[]{:S(2)}) collective-permute-start(bf16[576,256]{1,0:T(8,128)(2,1)} %get-tuple-element.11.refs_1_), channel_id=1, source_target_pairs={{0,16},{16,0},{1,17},{17,1},{2,18},{18,2},{3,19},{19,3},{4,20},{20... | collective-permute-start | bytes 884744 | tf_op jit(solution)/shard_map/ppermute | solution.py:189
  31.4 7.7 %all-to-all-done = bf16[128,8,128]{2,1,0:T(8,128)(2,1)S(1)} async-done(((bf16[128,8,128]{2,1,0:T(8,128)(2,1)}), bf16[128,8,128]{2,1,0:T(8,128)(2,1)S(1)}, u32[]{:S(2)}, u32[]{:S(2)}) %all-to-all-start) | async-done | bytes 262176 | tf_op jit(solution)/shard_map/all_to_all | solution.py:199
  39.1 3.5 %all-to-all-start.1 = ((bf16[16,2,16,256]{3,2,1,0:T(8,128)(2,1)}), bf16[16,2,16,256]{3,2,1,0:T(8,128)(2,1)S(1)}, u32[]{:S(2)}, u32[]{:S(2)}) async-start(bf16[16,2,16,256]{3,2,1,0:T(8,128)(2,1)} %get-tuple-element.13), calls=%async_computation.1 | async-start | bytes 524288 | tf_op jit(solution)/shard_map/all_to_all | solution.py:210
  42.6 0.0 copy-done.1
  42.6 1.9 %collective-permute-start.2 = (bf16[576,256]{1,0:T(8,128)(2,1)S(1)}, bf16[576,256]{1,0:T(8,128)(2,1)S(1)}, u32[]{:S(2)}, u32[]{:S(2)}) collective-permute-start(bf16[576,256]{1,0:T(8,128)(2,1)S(1)} %copy-done.1), channel_id=1, source_target_pairs={{0,1},{1,0},{2,3},{3,2},{4,5},{5,4},{6,7},{7,6},{8,9},{9,8},{10,11... | collective-permute-start | bytes 884744 | tf_op jit(solution)/shard_map/ppermute | solution.py:190
  44.6 2.4 %collective-permute-start.3 = (bf16[576,256]{1,0:T(8,128)(2,1)}, bf16[576,256]{1,0:T(8,128)(2,1)S(1)}, u32[]{:S(2)}, u32[]{:S(2)}) collective-permute-start(bf16[576,256]{1,0:T(8,128)(2,1)} %get-tuple-element.11.refs_1_), channel_id=1, source_target_pairs={{0,1},{1,0},{2,3},{3,2},{4,5},{5,4},{6,7},{7,6},{8,9},{9,8},{10,11... | collective-permute-start | bytes 884744 | tf_op jit(solution)/shard_map/ppermute | solution.py:190
  47.0 0.0 collective-permute-done.refs_2_
  47.0 1.9 %collective-permute-start.4 = (bf16[576,256]{1,0:T(8,128)(2,1)S(1)}, bf16[576,256]{1,0:T(8,128)(2,1)S(1)}, u32[]{:S(2)}, u32[]{:S(2)}) collective-permute-start(bf16[576,256]{1,0:T(8,128)(2,1)S(1)} %collective-permute-done.refs_2_), channel_id=1, source_target_pairs={{0,1},{1,0},{2,3},{3,2},{4,5},{5,4},{6,7},{7,6},{8,9},{9,8},{10,11... | collective-permute-start | bytes 884744 | tf_op jit(solution)/shard_map/ppermute | solution.py:191
  48.9 0.0 collective-permute-done.1.refs_3_
  48.9 2.4 %collective-permute-start.5 = (bf16[576,256]{1,0:T(8,128)(2,1)S(1)}, bf16[576,256]{1,0:T(8,128)(2,1)S(1)}, u32[]{:S(2)}, u32[]{:S(2)}) collective-permute-start(bf16[576,256]{1,0:T(8,128)(2,1)S(1)} %collective-permute-done.1.refs_3_), channel_id=1, source_target_pairs={{0,1},{1,0},{2,3},{3,2},{4,5},{5,4},{6,7},{7,6},{8,9},{9,8},{10,11... | collective-permute-start | bytes 884744 | tf_op jit(solution)/shard_map/ppermute | solution.py:191
  52.0 0.0 collective-permute-done.2.refs_4_
  52.0 0.0 collective-permute-done.3.refs_5_
  52.0 0.0 collective-permute-done.4.refs_6_
  52.0 0.5 collective-permute-done.5.refs_7_
  52.5 1.0 %copy-done.2 = bf16[576,256]{1,0:T(8,128)(2,1)S(1)} copy-done((bf16[576,256]{1,0:T(8,128)(2,1)S(1)}, bf16[576,256]{1,0:T(8,128)(2,1)}, u32[]{:S(2)}) %copy-start.2) | copy-done | bytes 294936
  53.5 2.8 %attend.1 = bf16[1280,128]{1,0:T(8,128)(2,1)} custom-call(s32[1]{0:T(128)S(6)} %copy.9.evict_ref, bf16[1024,128]{1,0:T(8,128)(2,1)S(1)} %bitcast.7, bf16[576,256]{1,0:T(8,128)(2,1)S(1)} %copy-done.1, bf16[576,256]{1,0:T(8,128)(2,1)S(1)} %copy-done.2, bf16[576,256]{1,0:T(8,128)(2,1)S(1)} %collective-permute-done.refs_2_, ...), custom_call_target="tpu_custom_call" | custom-call | tf_op jit(solution)/shard_map/attend/pallas_call | solution.py:202
  56.3 0.0 all-to-all-done.1.near_ref
  56.3 13.0 %all-to-all-start.2 = ((bf16[640,2,128]{2,1,0:T(2,128)(2,1)}), bf16[640,2,128]{2,1,0:T(2,128)(2,1)S(1)}, u32[]{:S(2)}, u32[]{:S(2)}) async-start(bf16[640,2,128]{2,1,0:T(2,128)(2,1)} %bitcast.3), calls=%async_computation.2 | async-start | bytes 655360 | tf_op jit(solution)/shard_map/all_to_all | solution.py:212
  69.3 3.4 %collective-permute-start.6 = (bf16[16,2,16,256]{3,2,1,0:T(8,128)(2,1)S(1)}, bf16[16,2,16,256]{3,2,1,0:T(8,128)(2,1)S(1)}, u32[]{:S(2)}, u32[]{:S(2)}) collective-permute-start(bf16[16,2,16,256]{3,2,1,0:T(8,128)(2,1)S(1)} %all-to-all-done.1.near_ref), channel_id=1, source_target_pairs={{0,16},{16,0},{1,17},{17,1},{2,18},{18,2},{3,19},{19,3},{4,20},{20... | collective-permute-start | bytes 786440 | tf_op jit(solution)/shard_map/ppermute | solution.py:222
  72.7 12.4 %collective-permute-done.6.far_ref = bf16[16,2,16,256]{3,2,1,0:T(8,128)(2,1)S(1)} collective-permute-done((bf16[16,2,16,256]{3,2,1,0:T(8,128)(2,1)S(1)}, bf16[16,2,16,256]{3,2,1,0:T(8,128)(2,1)S(1)}, u32[]{:S(2)}, u32[]{:S(2)}) %collective-permute-start.6) | collective-permute-done | bytes 262176 | tf_op jit(solution)/shard_map/ppermute | solution.py:222
  85.1 0.0 copy-done
  85.1 0.8 renew_cache.1
  85.9 1.8 %all-to-all-done.2 = bf16[640,2,128]{2,1,0:T(2,128)(2,1)S(1)} async-done(((bf16[640,2,128]{2,1,0:T(2,128)(2,1)}), bf16[640,2,128]{2,1,0:T(2,128)(2,1)S(1)}, u32[]{:S(2)}, u32[]{:S(2)}) %all-to-all-start.2) | async-done | bytes 327712 | tf_op jit(solution)/shard_map/all_to_all | solution.py:212
  87.7 1.1 %combine.1 = bf16[2,4096]{1,0:T(2,128)(2,1)} custom-call(bf16[1280,128]{1,0:T(8,128)(2,1)S(1)} %bitcast.6), custom_call_target="tpu_custom_call" | custom-call | tf_op jit(solution)/shard_map/combine/pallas_call | solution.py:215
  (3 shorter events, 0.0 us)
Async XLA Ops:
  0.6 0.7 copy-start.3
  1.3 0.7 copy-start.4
  2.9 36.2 %all-to-all-start = ((bf16[128,8,128]{2,1,0:T(8,128)(2,1)}), bf16[128,8,128]{2,1,0:T(8,128)(2,1)S(1)}, u32[]{:S(2)}, u32[]{:S(2)}) async-start(bf16[128,8,128]{2,1,0:T(8,128)(2,1)} %bitcast.1), calls=%async_computation | async-start | bytes 524288 | tf_op jit(solution)/shard_map/all_to_all | solution.py:199
  25.4 17.3 %copy-start.1 = (bf16[576,256]{1,0:T(8,128)(2,1)S(1)}, bf16[576,256]{1,0:T(8,128)(2,1)}, u32[]{:S(2)}) copy-start(bf16[576,256]{1,0:T(8,128)(2,1)} %get-tuple-element.10.refs_0_) | copy-start | bytes 884740
  25.4 21.6 %collective-permute-start = (bf16[576,256]{1,0:T(8,128)(2,1)}, bf16[576,256]{1,0:T(8,128)(2,1)S(1)}, u32[]{:S(2)}, u32[]{:S(2)}) collective-permute-start(bf16[576,256]{1,0:T(8,128)(2,1)} %get-tuple-element.10.refs_0_), channel_id=1, source_target_pairs={{0,16},{16,0},{1,17},{17,1},{2,18},{18,2},{3,19},{19,3},{4,20},{20... | collective-permute-start | bytes 884744 | tf_op jit(solution)/shard_map/ppermute | solution.py:189
  28.9 20.0 %collective-permute-start.1 = (bf16[576,256]{1,0:T(8,128)(2,1)}, bf16[576,256]{1,0:T(8,128)(2,1)S(1)}, u32[]{:S(2)}, u32[]{:S(2)}) collective-permute-start(bf16[576,256]{1,0:T(8,128)(2,1)} %get-tuple-element.11.refs_1_), channel_id=1, source_target_pairs={{0,16},{16,0},{1,17},{17,1},{2,18},{18,2},{3,19},{19,3},{4,20},{20... | collective-permute-start | bytes 884744 | tf_op jit(solution)/shard_map/ppermute | solution.py:189
  39.1 17.2 %all-to-all-start.1 = ((bf16[16,2,16,256]{3,2,1,0:T(8,128)(2,1)}), bf16[16,2,16,256]{3,2,1,0:T(8,128)(2,1)S(1)}, u32[]{:S(2)}, u32[]{:S(2)}) async-start(bf16[16,2,16,256]{3,2,1,0:T(8,128)(2,1)} %get-tuple-element.13), calls=%async_computation.1 | async-start | bytes 524288 | tf_op jit(solution)/shard_map/all_to_all | solution.py:210
  42.6 9.4 %collective-permute-start.2 = (bf16[576,256]{1,0:T(8,128)(2,1)S(1)}, bf16[576,256]{1,0:T(8,128)(2,1)S(1)}, u32[]{:S(2)}, u32[]{:S(2)}) collective-permute-start(bf16[576,256]{1,0:T(8,128)(2,1)S(1)} %copy-done.1), channel_id=1, source_target_pairs={{0,1},{1,0},{2,3},{3,2},{4,5},{5,4},{6,7},{7,6},{8,9},{9,8},{10,11... | collective-permute-start | bytes 884744 | tf_op jit(solution)/shard_map/ppermute | solution.py:190
  44.6 7.4 %collective-permute-start.3 = (bf16[576,256]{1,0:T(8,128)(2,1)}, bf16[576,256]{1,0:T(8,128)(2,1)S(1)}, u32[]{:S(2)}, u32[]{:S(2)}) collective-permute-start(bf16[576,256]{1,0:T(8,128)(2,1)} %get-tuple-element.11.refs_1_), channel_id=1, source_target_pairs={{0,1},{1,0},{2,3},{3,2},{4,5},{5,4},{6,7},{7,6},{8,9},{9,8},{10,11... | collective-permute-start | bytes 884744 | tf_op jit(solution)/shard_map/ppermute | solution.py:190
  47.0 5.0 %collective-permute-start.4 = (bf16[576,256]{1,0:T(8,128)(2,1)S(1)}, bf16[576,256]{1,0:T(8,128)(2,1)S(1)}, u32[]{:S(2)}, u32[]{:S(2)}) collective-permute-start(bf16[576,256]{1,0:T(8,128)(2,1)S(1)} %collective-permute-done.refs_2_), channel_id=1, source_target_pairs={{0,1},{1,0},{2,3},{3,2},{4,5},{5,4},{6,7},{7,6},{8,9},{9,8},{10,11... | collective-permute-start | bytes 884744 | tf_op jit(solution)/shard_map/ppermute | solution.py:191
  48.9 3.6 %collective-permute-start.5 = (bf16[576,256]{1,0:T(8,128)(2,1)S(1)}, bf16[576,256]{1,0:T(8,128)(2,1)S(1)}, u32[]{:S(2)}, u32[]{:S(2)}) collective-permute-start(bf16[576,256]{1,0:T(8,128)(2,1)S(1)} %collective-permute-done.1.refs_3_), channel_id=1, source_target_pairs={{0,1},{1,0},{2,3},{3,2},{4,5},{5,4},{6,7},{7,6},{8,9},{9,8},{10,11... | collective-permute-start | bytes 884744 | tf_op jit(solution)/shard_map/ppermute | solution.py:191
  52.5 1.0 %copy-start.2 = (bf16[576,256]{1,0:T(8,128)(2,1)S(1)}, bf16[576,256]{1,0:T(8,128)(2,1)}, u32[]{:S(2)}) copy-start(bf16[576,256]{1,0:T(8,128)(2,1)} %get-tuple-element.11.refs_1_) | copy-start | bytes 884740
  56.3 28.8 %copy-start = (bf16[1,2,512,256]{3,2,1,0:T(8,128)(2,1)S(1)}, bf16[1,2,512,256]{3,2,1,0:T(8,128)(2,1)}, u32[]{:S(2)}) copy-start(bf16[1,2,512,256]{3,2,1,0:T(8,128)(2,1)} %cache_ref.3) | copy-start | bytes 1572868
  56.3 31.4 %all-to-all-start.2 = ((bf16[640,2,128]{2,1,0:T(2,128)(2,1)}), bf16[640,2,128]{2,1,0:T(2,128)(2,1)S(1)}, u32[]{:S(2)}, u32[]{:S(2)}) async-start(bf16[640,2,128]{2,1,0:T(2,128)(2,1)} %bitcast.3), calls=%async_computation.2 | async-start | bytes 655360 | tf_op jit(solution)/shard_map/all_to_all | solution.py:212
  69.3 15.8 %collective-permute-start.6 = (bf16[16,2,16,256]{3,2,1,0:T(8,128)(2,1)S(1)}, bf16[16,2,16,256]{3,2,1,0:T(8,128)(2,1)S(1)}, u32[]{:S(2)}, u32[]{:S(2)}) collective-permute-start(bf16[16,2,16,256]{3,2,1,0:T(8,128)(2,1)S(1)} %all-to-all-done.1.near_ref), channel_id=1, source_target_pairs={{0,16},{16,0},{1,17},{17,1},{2,18},{18,2},{3,19},{19,3},{4,20},{20... | collective-permute-start | bytes 786440 | tf_op jit(solution)/shard_map/ppermute | solution.py:222

commit v3 on v2

--- a/solution.py
+++ b/solution.py
@@ -206,6 +206,7 @@
         [pltpu.VMEM((tokens * PARTS, HD), f32), pltpu.VMEM((tokens * BACK, HD), f32)],
         name="attend",
     )(evict, recv, *pack, *far, *side, *cross)
+    _, copies = lax.optimization_barrier((side, copies))
     _, copies = lax.optimization_barrier((recv, copies))
     near = lax.all_to_all(copies, "ca", split_axis=0, concat_axis=0, tiled=True)
     parts, near = lax.optimization_barrier((parts, near))

time: 89.5 us -> 92.8 us (1.037)
  starting transfers between devices: 54.4 us -> 59.2 us
  waiting for transfers between devices: 22.4 us -> 20.8 us
    all_to_all x1, waiting for transfers between devices: 7.72 us -> 3.35 us  [body(): lax.all_to_all(message.reshape(tokens, PARTS, HD), ('ca', 'ha'), split_ax...]
    all_to_all x1, waiting for transfers between devices: 0.01 us -> 2.89 us  [body(): near = lax.all_to_all(copies, 'ca', split_axis=0, concat_axis=0, tiled=True)]
    all_to_all x1, starting transfers between devices: 13 us -> 15.4 us  [body(): lax.all_to_all(parts.reshape(tokens * BACK // 2, 2, HD), ('ca', 'ha'), sp...]
    all_to_all x1, starting transfers between devices: 3.53 us -> 5.63 us  [body(): near = lax.all_to_all(copies, 'ca', split_axis=0, concat_axis=0, tiled=True)]
  transfers between devices with their start and end apart: 10 -> 10, of which waited for: 4 -> 6; matrix products, arithmetic and copies ran while one was open for 0% -> 0% of each run, Pallas kernels for 6% -> 6%
where the time goes in v3:
time: 92.8 us; the launch traced here: 92 us
  starting transfers between devices  59.2 us (64%)
  waiting for transfers between devices  20.8 us (22%)
  Pallas kernels  7.5 us (8%)
  local copies, waits for them, and re-layouts  2.4 us (3%)
  between operations  2.07 us (2%)
    all_to_all x1, starting transfers between devices, body(): lax.all_to_all(message.reshape(tokens, PARTS, HD), ('ca', 'ha'), split_ax...  19.8 us
    all_to_all x1, starting transfers between devices, body(): lax.all_to_all(parts.reshape(tokens * BACK // 2, 2, HD), ('ca', 'ha'), sp...  15.4 us
    ppermute x1, waiting for transfers between devices, body(): other = lax.ppermute(near, 'cb', swap)  11.9 us
    ppermute x2, starting transfers between devices, body(): far = [lax.ppermute(array, 'cb', swap) for array in pack]  5.84 us
    all_to_all x1, starting transfers between devices, body(): near = lax.all_to_all(copies, 'ca', split_axis=0, concat_axis=0, tiled=True)  5.63 us
    ppermute x2, starting transfers between devices, body(): side = [lax.ppermute(array, 'hb', swap) for array in pack]  4.46 us
    ppermute x1, starting transfers between devices, body(): other = lax.ppermute(near, 'cb', swap)  4.29 us
    ppermute x2, starting transfers between devices, body(): cross = [lax.ppermute(array, 'hb', swap) for array in far]  3.83 us
  transfers between devices with their start and end apart: 10, of which 6 were waited for; matrix products, arithmetic and copies ran while one was open for 0% of the time, Pallas kernels for 6%

profile of v3, /device:TPU:6, one launch (start us, length us, event | category | flops | bytes accessed | tf_op | source)
XLA Modules:
  0.0 92.0 jit_solution(1251698451133536798)
XLA Ops:
  0.6 0.0 copy-start.3
  0.6 0.7 copy-done.3
  1.4 0.7 copy-done.4
  2.1 0.8 spread.1
  2.9 19.8 %all-to-all-start = ((bf16[128,8,128]{2,1,0:T(8,128)(2,1)}), bf16[128,8,128]{2,1,0:T(8,128)(2,1)S(1)}, u32[]{:S(2)}, u32[]{:S(2)}) async-start(bf16[128,8,128]{2,1,0:T(8,128)(2,1)} %bitcast.1), calls=%async_computation | async-start | bytes 524288 | tf_op jit(solution)/shard_map/all_to_all | solution.py:199
  23.4 2.0 %pack.1 = (bf16[576,256]{1,0:T(8,128)(2,1)}, bf16[576,256]{1,0:T(8,128)(2,1)}) custom-call(s32[1]{0:T(128)S(6)} %copy.8.length_ref, bf16[1,2,512,256]{3,2,1,0:T(8,128)(2,1)} %cache_ref.3, bf16[2,2,16,256]{3,2,1,0:T(8,128)(2,1)} %own_ref.1, bf16[2,16,256]{2,1,0:T(8,128)(2,1)} %clean_ref.3), custom_call_target="tpu_custom_call" | custom-call | tf_op jit(solution)/shard_map/pack/pallas_call | solution.py:181
  25.4 0.0 copy-start.1
  25.4 2.1 %collective-permute-start.2 = (bf16[576,256]{1,0:T(8,128)(2,1)}, bf16[576,256]{1,0:T(8,128)(2,1)S(1)}, u32[]{:S(2)}, u32[]{:S(2)}) collective-permute-start(bf16[576,256]{1,0:T(8,128)(2,1)} %get-tuple-element.11.refs_0_), channel_id=1, source_target_pairs={{0,1},{1,0},{2,3},{3,2},{4,5},{5,4},{6,7},{7,6},{8,9},{9,8},{10,11... | collective-permute-start | bytes 884744 | tf_op jit(solution)/shard_map/ppermute | solution.py:190
  27.5 2.4 %collective-permute-start.3 = (bf16[576,256]{1,0:T(8,128)(2,1)}, bf16[576,256]{1,0:T(8,128)(2,1)S(1)}, u32[]{:S(2)}, u32[]{:S(2)}) collective-permute-start(bf16[576,256]{1,0:T(8,128)(2,1)} %get-tuple-element.12.refs_1_), channel_id=1, source_target_pairs={{0,1},{1,0},{2,3},{3,2},{4,5},{5,4},{6,7},{7,6},{8,9},{9,8},{10,11... | collective-permute-start | bytes 884744 | tf_op jit(solution)/shard_map/ppermute | solution.py:190
  29.9 3.4 %collective-permute-start = (bf16[576,256]{1,0:T(8,128)(2,1)}, bf16[576,256]{1,0:T(8,128)(2,1)S(1)}, u32[]{:S(2)}, u32[]{:S(2)}) collective-permute-start(bf16[576,256]{1,0:T(8,128)(2,1)} %get-tuple-element.11.refs_0_), channel_id=1, source_target_pairs={{0,16},{16,0},{1,17},{17,1},{2,18},{18,2},{3,19},{19,3},{4,20},{20... | collective-permute-start | bytes 884744 | tf_op jit(solution)/shard_map/ppermute | solution.py:189
  33.3 2.5 %collective-permute-start.1 = (bf16[576,256]{1,0:T(8,128)(2,1)}, bf16[576,256]{1,0:T(8,128)(2,1)S(1)}, u32[]{:S(2)}, u32[]{:S(2)}) collective-permute-start(bf16[576,256]{1,0:T(8,128)(2,1)} %get-tuple-element.12.refs_1_), channel_id=1, source_target_pairs={{0,16},{16,0},{1,17},{17,1},{2,18},{18,2},{3,19},{19,3},{4,20},{20... | collective-permute-start | bytes 884744 | tf_op jit(solution)/shard_map/ppermute | solution.py:189
  35.7 0.0 collective-permute-done.2.refs_4_
  35.7 0.0 collective-permute-done.3.refs_5_
  35.7 3.4 %all-to-all-done = bf16[128,8,128]{2,1,0:T(8,128)(2,1)S(1)} async-done(((bf16[128,8,128]{2,1,0:T(8,128)(2,1)}), bf16[128,8,128]{2,1,0:T(8,128)(2,1)S(1)}, u32[]{:S(2)}, u32[]{:S(2)}) %all-to-all-start) | async-done | bytes 262176 | tf_op jit(solution)/shard_map/all_to_all | solution.py:199
  39.1 5.6 %all-to-all-start.1 = ((bf16[16,2,16,256]{3,2,1,0:T(8,128)(2,1)}), bf16[16,2,16,256]{3,2,1,0:T(8,128)(2,1)S(1)}, u32[]{:S(2)}, u32[]{:S(2)}) async-start(bf16[16,2,16,256]{3,2,1,0:T(8,128)(2,1)} %get-tuple-element.15), calls=%async_computation.1 | async-start | bytes 524288 | tf_op jit(solution)/shard_map/all_to_all | solution.py:211
  44.7 0.0 collective-permute-done.refs_2_
  44.7 1.9 %collective-permute-start.4 = (bf16[576,256]{1,0:T(8,128)(2,1)S(1)}, bf16[576,256]{1,0:T(8,128)(2,1)S(1)}, u32[]{:S(2)}, u32[]{:S(2)}) collective-permute-start(bf16[576,256]{1,0:T(8,128)(2,1)S(1)} %collective-permute-done.refs_2_), channel_id=1, source_target_pairs={{0,1},{1,0},{2,3},{3,2},{4,5},{5,4},{6,7},{7,6},{8,9},{9,8},{10,11... | collective-permute-start | bytes 884744 | tf_op jit(solution)/shard_map/ppermute | solution.py:191
  46.7 0.6 collective-permute-done.1.refs_3_
  47.3 1.9 %collective-permute-start.5 = (bf16[576,256]{1,0:T(8,128)(2,1)S(1)}, bf16[576,256]{1,0:T(8,128)(2,1)S(1)}, u32[]{:S(2)}, u32[]{:S(2)}) collective-permute-start(bf16[576,256]{1,0:T(8,128)(2,1)S(1)} %collective-permute-done.1.refs_3_), channel_id=1, source_target_pairs={{0,1},{1,0},{2,3},{3,2},{4,5},{5,4},{6,7},{7,6},{8,9},{9,8},{10,11... | collective-permute-start | bytes 884744 | tf_op jit(solution)/shard_map/ppermute | solution.py:191
  49.9 0.0 collective-permute-done.4.refs_6_
  49.9 0.9 collective-permute-done.5.refs_7_
  50.8 0.0 copy-done.1
  50.8 1.0 %copy-done.2 = bf16[576,256]{1,0:T(8,128)(2,1)S(1)} copy-done((bf16[576,256]{1,0:T(8,128)(2,1)S(1)}, bf16[576,256]{1,0:T(8,128)(2,1)}, u32[]{:S(2)}) %copy-start.2) | copy-done | bytes 294936
  51.7 2.8 %attend.1 = bf16[1280,128]{1,0:T(8,128)(2,1)} custom-call(s32[1]{0:T(128)S(6)} %copy.9.evict_ref, bf16[1024,128]{1,0:T(8,128)(2,1)S(1)} %bitcast.7, bf16[576,256]{1,0:T(8,128)(2,1)S(1)} %copy-done.1, bf16[576,256]{1,0:T(8,128)(2,1)S(1)} %copy-done.2, bf16[576,256]{1,0:T(8,128)(2,1)S(1)} %collective-permute-done.refs_2_, ...), custom_call_target="tpu_custom_call" | custom-call | tf_op jit(solution)/shard_map/attend/pallas_call | solution.py:202
  54.5 2.9 %all-to-all-done.1.near_ref = bf16[16,2,16,256]{3,2,1,0:T(8,128)(2,1)S(1)} async-done(((bf16[16,2,16,256]{3,2,1,0:T(8,128)(2,1)}), bf16[16,2,16,256]{3,2,1,0:T(8,128)(2,1)S(1)}, u32[]{:S(2)}, u32[]{:S(2)}) %all-to-all-start.1) | async-done | bytes 262176 | tf_op jit(solution)/shard_map/all_to_all | solution.py:211
  57.4 15.4 %all-to-all-start.2 = ((bf16[640,2,128]{2,1,0:T(2,128)(2,1)}), bf16[640,2,128]{2,1,0:T(2,128)(2,1)S(1)}, u32[]{:S(2)}, u32[]{:S(2)}) async-start(bf16[640,2,128]{2,1,0:T(2,128)(2,1)} %bitcast.3), calls=%async_computation.2 | async-start | bytes 655360 | tf_op jit(solution)/shard_map/all_to_all | solution.py:213
  72.8 4.3 %collective-permute-start.6 = (bf16[16,2,16,256]{3,2,1,0:T(8,128)(2,1)S(1)}, bf16[16,2,16,256]{3,2,1,0:T(8,128)(2,1)S(1)}, u32[]{:S(2)}, u32[]{:S(2)}) collective-permute-start(bf16[16,2,16,256]{3,2,1,0:T(8,128)(2,1)S(1)} %all-to-all-done.1.near_ref), channel_id=1, source_target_pairs={{0,16},{16,0},{1,17},{17,1},{2,18},{18,2},{3,19},{19,3},{4,20},{20... | collective-permute-start | bytes 786440 | tf_op jit(solution)/shard_map/ppermute | solution.py:223
  77.1 11.9 %collective-permute-done.6.far_ref = bf16[16,2,16,256]{3,2,1,0:T(8,128)(2,1)S(1)} collective-permute-done((bf16[16,2,16,256]{3,2,1,0:T(8,128)(2,1)S(1)}, bf16[16,2,16,256]{3,2,1,0:T(8,128)(2,1)S(1)}, u32[]{:S(2)}, u32[]{:S(2)}) %collective-permute-start.6) | collective-permute-done | bytes 262176 | tf_op jit(solution)/shard_map/ppermute | solution.py:223
  88.9 0.0 copy-done
  89.0 0.8 renew_cache.1
  89.8 1.1 %all-to-all-done.2 = bf16[640,2,128]{2,1,0:T(2,128)(2,1)S(1)} async-done(((bf16[640,2,128]{2,1,0:T(2,128)(2,1)}), bf16[640,2,128]{2,1,0:T(2,128)(2,1)S(1)}, u32[]{:S(2)}, u32[]{:S(2)}) %all-to-all-start.2) | async-done | bytes 327712 | tf_op jit(solution)/shard_map/all_to_all | solution.py:213
  90.9 1.1 %combine.1 = bf16[2,4096]{1,0:T(2,128)(2,1)} custom-call(bf16[1280,128]{1,0:T(8,128)(2,1)S(1)} %bitcast.6), custom_call_target="tpu_custom_call" | custom-call | tf_op jit(solution)/shard_map/combine/pallas_call | solution.py:216
  (3 shorter events, 0.0 us)
Async XLA Ops:
  0.6 0.7 copy-start.3
  1.3 0.7 copy-start.4
  2.9 36.2 %all-to-all-start = ((bf16[128,8,128]{2,1,0:T(8,128)(2,1)}), bf16[128,8,128]{2,1,0:T(8,128)(2,1)S(1)}, u32[]{:S(2)}, u32[]{:S(2)}) async-start(bf16[128,8,128]{2,1,0:T(8,128)(2,1)} %bitcast.1), calls=%async_computation | async-start | bytes 524288 | tf_op jit(solution)/shard_map/all_to_all | solution.py:199
  25.4 25.4 %copy-start.1 = (bf16[576,256]{1,0:T(8,128)(2,1)S(1)}, bf16[576,256]{1,0:T(8,128)(2,1)}, u32[]{:S(2)}) copy-start(bf16[576,256]{1,0:T(8,128)(2,1)} %get-tuple-element.11.refs_0_) | copy-start | bytes 884740
  25.4 10.3 %collective-permute-start.2 = (bf16[576,256]{1,0:T(8,128)(2,1)}, bf16[576,256]{1,0:T(8,128)(2,1)S(1)}, u32[]{:S(2)}, u32[]{:S(2)}) collective-permute-start(bf16[576,256]{1,0:T(8,128)(2,1)} %get-tuple-element.11.refs_0_), channel_id=1, source_target_pairs={{0,1},{1,0},{2,3},{3,2},{4,5},{5,4},{6,7},{7,6},{8,9},{9,8},{10,11... | collective-permute-start | bytes 884744 | tf_op jit(solution)/shard_map/ppermute | solution.py:190
  27.5 8.3 %collective-permute-start.3 = (bf16[576,256]{1,0:T(8,128)(2,1)}, bf16[576,256]{1,0:T(8,128)(2,1)S(1)}, u32[]{:S(2)}, u32[]{:S(2)}) collective-permute-start(bf16[576,256]{1,0:T(8,128)(2,1)} %get-tuple-element.12.refs_1_), channel_id=1, source_target_pairs={{0,1},{1,0},{2,3},{3,2},{4,5},{5,4},{6,7},{7,6},{8,9},{9,8},{10,11... | collective-permute-start | bytes 884744 | tf_op jit(solution)/shard_map/ppermute | solution.py:190
  29.9 14.9 %collective-permute-start = (bf16[576,256]{1,0:T(8,128)(2,1)}, bf16[576,256]{1,0:T(8,128)(2,1)S(1)}, u32[]{:S(2)}, u32[]{:S(2)}) collective-permute-start(bf16[576,256]{1,0:T(8,128)(2,1)} %get-tuple-element.11.refs_0_), channel_id=1, source_target_pairs={{0,16},{16,0},{1,17},{17,1},{2,18},{18,2},{3,19},{19,3},{4,20},{20... | collective-permute-start | bytes 884744 | tf_op jit(solution)/shard_map/ppermute | solution.py:189
  33.3 14.1 %collective-permute-start.1 = (bf16[576,256]{1,0:T(8,128)(2,1)}, bf16[576,256]{1,0:T(8,128)(2,1)S(1)}, u32[]{:S(2)}, u32[]{:S(2)}) collective-permute-start(bf16[576,256]{1,0:T(8,128)(2,1)} %get-tuple-element.12.refs_1_), channel_id=1, source_target_pairs={{0,16},{16,0},{1,17},{17,1},{2,18},{18,2},{3,19},{19,3},{4,20},{20... | collective-permute-start | bytes 884744 | tf_op jit(solution)/shard_map/ppermute | solution.py:189
  39.1 18.3 %all-to-all-start.1 = ((bf16[16,2,16,256]{3,2,1,0:T(8,128)(2,1)}), bf16[16,2,16,256]{3,2,1,0:T(8,128)(2,1)S(1)}, u32[]{:S(2)}, u32[]{:S(2)}) async-start(bf16[16,2,16,256]{3,2,1,0:T(8,128)(2,1)} %get-tuple-element.15), calls=%async_computation.1 | async-start | bytes 524288 | tf_op jit(solution)/shard_map/all_to_all | solution.py:211
  44.7 5.1 %collective-permute-start.4 = (bf16[576,256]{1,0:T(8,128)(2,1)S(1)}, bf16[576,256]{1,0:T(8,128)(2,1)S(1)}, u32[]{:S(2)}, u32[]{:S(2)}) collective-permute-start(bf16[576,256]{1,0:T(8,128)(2,1)S(1)} %collective-permute-done.refs_2_), channel_id=1, source_target_pairs={{0,1},{1,0},{2,3},{3,2},{4,5},{5,4},{6,7},{7,6},{8,9},{9,8},{10,11... | collective-permute-start | bytes 884744 | tf_op jit(solution)/shard_map/ppermute | solution.py:191
  47.3 3.5 %collective-permute-start.5 = (bf16[576,256]{1,0:T(8,128)(2,1)S(1)}, bf16[576,256]{1,0:T(8,128)(2,1)S(1)}, u32[]{:S(2)}, u32[]{:S(2)}) collective-permute-start(bf16[576,256]{1,0:T(8,128)(2,1)S(1)} %collective-permute-done.1.refs_3_), channel_id=1, source_target_pairs={{0,1},{1,0},{2,3},{3,2},{4,5},{5,4},{6,7},{7,6},{8,9},{9,8},{10,11... | collective-permute-start | bytes 884744 | tf_op jit(solution)/shard_map/ppermute | solution.py:191
  50.8 1.0 %copy-start.2 = (bf16[576,256]{1,0:T(8,128)(2,1)S(1)}, bf16[576,256]{1,0:T(8,128)(2,1)}, u32[]{:S(2)}) copy-start(bf16[576,256]{1,0:T(8,128)(2,1)} %get-tuple-element.12.refs_1_) | copy-start | bytes 884740
  54.5 34.4 %copy-start = (bf16[1,2,512,256]{3,2,1,0:T(8,128)(2,1)S(1)}, bf16[1,2,512,256]{3,2,1,0:T(8,128)(2,1)}, u32[]{:S(2)}) copy-start(bf16[1,2,512,256]{3,2,1,0:T(8,128)(2,1)} %cache_ref.3) | copy-start | bytes 1572868
  57.4 33.5 %all-to-all-start.2 = ((bf16[640,2,128]{2,1,0:T(2,128)(2,1)}), bf16[640,2,128]{2,1,0:T(2,128)(2,1)S(1)}, u32[]{:S(2)}, u32[]{:S(2)}) async-start(bf16[640,2,128]{2,1,0:T(2,128)(2,1)} %bitcast.3), calls=%async_computation.2 | async-start | bytes 655360 | tf_op jit(solution)/shard_map/all_to_all | solution.py:213
  72.8 16.2 %collective-permute-start.6 = (bf16[16,2,16,256]{3,2,1,0:T(8,128)(2,1)S(1)}, bf16[16,2,16,256]{3,2,1,0:T(8,128)(2,1)S(1)}, u32[]{:S(2)}, u32[]{:S(2)}) collective-permute-start(bf16[16,2,16,256]{3,2,1,0:T(8,128)(2,1)S(1)} %all-to-all-done.1.near_ref), channel_id=1, source_target_pairs={{0,16},{16,0},{1,17},{17,1},{2,18},{18,2},{3,19},{19,3},{4,20},{20... | collective-permute-start | bytes 786440 | tf_op jit(solution)/shard_map/ppermute | solution.py:223

commit v4 on v0

--- a/solution.py
+++ b/solution.py
@@ -31,7 +31,7 @@
         copies_ref[dest] = clean_ref[...]
 
 
-def pack_kernel(length_ref, cache_ref, own_ref, clean_ref, pack_ref, digit_rows, sems):
+def pack_kernel(length_ref, cache_ref, own_ref, clean_ref, pack_ref, digit_rows, sems, meanwhile):
     span, rows = cache_ref.shape[2], clean_ref.shape[1]
     pieces = [(cache_ref.at[0, index], span) for index in range(2)]
     pieces += [(own_ref.at[step, index], rows) for step in range(2) for index in range(2)]
@@ -46,8 +46,18 @@
         copies.append(pltpu.make_async_copy(piece, pack_ref.at[pl.ds(place, count)], sems.at[number]))
         copies[-1].start()
         place += count
+    meanwhile()
     for copy in copies:
         copy.wait()
+
+
+def front_kernel(
+    length_ref, cache_ref, own_ref, far_clean_ref, q_ref, clean_ref, pack_ref, out_ref, copies_ref, digit_rows, sems, rows
+):
+    pack_kernel(
+        length_ref, cache_ref, own_ref, far_clean_ref, pack_ref, digit_rows, sems,
+        lambda: spread_kernel(q_ref, clean_ref, out_ref, copies_ref, rows),
+    )
 
 
 def attend_kernel(evict_ref, recv_ref, pack_ref, far_ref, side_ref, cross_ref, out_ref, wide, wide_out):
@@ -177,24 +187,25 @@
     bf16, f32 = jnp.bfloat16, jnp.float32
     shape = jax.ShapeDtypeStruct
     swap = [(0, 1), (1, 0)]
-    pack = call(
-        pack_kernel,
-        shape((2 * span + 7 * rows, width), bf16),
-        [SMEM] + [HBM] * 3,
-        [pltpu.VMEM((rows, width), bf16), pltpu.SemaphoreType.DMA((9,))],
-        name="pack",
+    pack, message, copies = call(
+        front_kernel,
+        (
+            shape((2 * span + 7 * rows, width), bf16),
+            shape((tokens * PARTS, HD), bf16),
+            shape((pairs,) + clean_kv.shape, bf16),
+        ),
+        [SMEM] + [HBM] * 3 + [VMEM] * 2,
+        [
+            pltpu.VMEM((rows, width), bf16),
+            pltpu.SemaphoreType.DMA((9,)),
+            pltpu.VMEM((chips * PARTS, HD), f32),
+        ],
+        name="front",
         limit=60,
-    )(lengths, cache_kv, own_kv, clean_kv)
+    )(lengths, cache_kv, own_kv, clean_kv, queries.reshape(steps, features), clean_kv)
     far = lax.ppermute(pack, "cb", swap)
     side = lax.ppermute(pack, "hb", swap)
     cross = lax.ppermute(far, "hb", swap)
-    message, copies = call(
-        spread_kernel,
-        (shape((tokens * PARTS, HD), bf16), shape((pairs,) + clean_kv.shape, bf16)),
-        [VMEM] * 2,
-        [pltpu.VMEM((chips * PARTS, HD), f32)],
-        name="spread",
-    )(queries.reshape(steps, features), clean_kv)
     recv = lax.all_to_all(
         message.reshape(tokens, PARTS, HD), ("ca", "ha"), split_axis=0, concat_axis=0, tiled=True
     ).reshape(tokens * PARTS, HD)

time: 84.3 us -> 84.6 us (level)
    pallas_call x2 -> x1, Pallas kernels: 2.78 us -> 2.84 us  [body(): call(front_kernel, (shape((2 * span + 7 * rows, width), bf16), shape((tok...]
  transfers between devices with their start and end apart: 7 -> 7, of which waited for: 4 -> 4; matrix products, arithmetic and copies ran while one was open for 0% -> 0% of each run, Pallas kernels for 5% -> 4%
where the time goes in v4:
time: 84.6 us; the launch traced here: 83.9 us
  starting transfers between devices  41.8 us (49%)
  waiting for transfers between devices  32.5 us (38%)
  Pallas kernels  7.62 us (9%)
  between operations  2.03 us (2%)
    all_to_all x1, starting transfers between devices, body(): lax.all_to_all(message.reshape(tokens, PARTS, HD), ('ca', 'ha'), split_ax...  19 us
    all_to_all x1, waiting for transfers between devices, body(): lax.all_to_all(message.reshape(tokens, PARTS, HD), ('ca', 'ha'), split_ax...  11.7 us
    ppermute x1, waiting for transfers between devices, body(): other = lax.ppermute(near, 'cb', swap)  10.2 us
    all_to_all x1, waiting for transfers between devices, body(): near = lax.all_to_all(copies, 'ca', split_axis=0, concat_axis=0, tiled=True)  8.18 us
    all_to_all x1, starting transfers between devices, body(): lax.all_to_all(parts.reshape(tokens * BACK // 2, 2, HD), ('ca', 'ha'), sp...  8.04 us
    ppermute x1, starting transfers between devices, body(): far = lax.ppermute(pack, 'cb', swap)  4.41 us
    all_to_all x1, starting transfers between devices, body(): near = lax.all_to_all(copies, 'ca', split_axis=0, concat_axis=0, tiled=True)  3.53 us
    pallas_call x1, Pallas kernels, body(): call(attend_kernel, shape((tokens * BACK, HD), bf16), [SMEM] + [VMEM] * 5...  2.86 us
  transfers between devices with their start and end apart: 7, of which 4 were waited for; matrix products, arithmetic and copies ran while one was open for 0% of the time, Pallas kernels for 4%

profile of v4, /device:TPU:6, one launch (start us, length us, event | category | flops | bytes accessed | tf_op | source)
XLA Modules:
  0.0 83.9 jit_solution(12946399369005842536)
XLA Ops:
  1.3 2.8 %front.1 = (bf16[1136,256]{1,0:T(8,128)(2,1)}, bf16[1024,128]{1,0:T(8,128)(2,1)}, bf16[16,2,16,256]{3,2,1,0:T(8,128)(2,1)}) custom-call(s32[1]{0:T(128)S(6)} %copy.8.length_ref, bf16[1,2,512,256]{3,2,1,0:T(8,128)(2,1)} %cache_ref.3, bf16[2,2,16,256]{3,2,1,0:T(8,128)(2,1)} %own_ref.1, bf16[2,16,256]{2,1,0:T(8,128)(2,1)} %clean_ref.1, ...), custom_call_target="tpu_custom_call" | custom-call | tf_op jit(solution)/shard_map/front/pallas_call | solution.py:190
  4.1 0.0 copy-start.1
  4.1 4.4 %collective-permute-start = (bf16[1136,256]{1,0:T(8,128)(2,1)}, bf16[1136,256]{1,0:T(8,128)(2,1)S(1)}, u32[]{:S(2)}, u32[]{:S(2)}) collective-permute-start(bf16[1136,256]{1,0:T(8,128)(2,1)} %get-tuple-element.9.pack_ref), channel_id=1, source_target_pairs={{0,16},{16,0},{1,17},{17,1},{2,18},{18,2},{3,19},{19,3},{4,20},{20... | collective-permute-start | bytes 1744904 | tf_op jit(solution)/shard_map/ppermute | solution.py:206
  8.5 19.0 %all-to-all-start = ((bf16[128,8,128]{2,1,0:T(8,128)(2,1)}), bf16[128,8,128]{2,1,0:T(8,128)(2,1)S(1)}, u32[]{:S(2)}, u32[]{:S(2)}) async-start(bf16[128,8,128]{2,1,0:T(8,128)(2,1)} %bitcast.8), calls=%async_computation | async-start | bytes 524288 | tf_op jit(solution)/shard_map/all_to_all | solution.py:209
  27.5 1.9 %collective-permute-start.1 = (bf16[1136,256]{1,0:T(8,128)(2,1)}, bf16[1136,256]{1,0:T(8,128)(2,1)S(1)}, u32[]{:S(2)}, u32[]{:S(2)}) collective-permute-start(bf16[1136,256]{1,0:T(8,128)(2,1)} %get-tuple-element.9.pack_ref), channel_id=1, source_target_pairs={{0,1},{1,0},{2,3},{3,2},{4,5},{5,4},{6,7},{7,6},{8,9},{9,8},{10,11... | collective-permute-start | bytes 1744904 | tf_op jit(solution)/shard_map/ppermute | solution.py:207
  29.4 0.0 collective-permute-done.far_ref
  29.5 2.4 %collective-permute-start.2 = (bf16[1136,256]{1,0:T(8,128)(2,1)S(1)}, bf16[1136,256]{1,0:T(8,128)(2,1)S(1)}, u32[]{:S(2)}, u32[]{:S(2)}) collective-permute-start(bf16[1136,256]{1,0:T(8,128)(2,1)S(1)} %collective-permute-done.far_ref), channel_id=1, source_target_pairs={{0,1},{1,0},{2,3},{3,2},{4,5},{5,4},{6,7},{7,6},{8,9},{9,8},{10,11... | collective-permute-start | bytes 1744904 | tf_op jit(solution)/shard_map/ppermute | solution.py:208
  31.9 11.7 %all-to-all-done = bf16[128,8,128]{2,1,0:T(8,128)(2,1)S(1)} async-done(((bf16[128,8,128]{2,1,0:T(8,128)(2,1)}), bf16[128,8,128]{2,1,0:T(8,128)(2,1)S(1)}, u32[]{:S(2)}, u32[]{:S(2)}) %all-to-all-start) | async-done | bytes 262176 | tf_op jit(solution)/shard_map/all_to_all | solution.py:209
  43.6 3.5 %all-to-all-start.1 = ((bf16[16,2,16,256]{3,2,1,0:T(8,128)(2,1)}), bf16[16,2,16,256]{3,2,1,0:T(8,128)(2,1)S(1)}, u32[]{:S(2)}, u32[]{:S(2)}) async-start(bf16[16,2,16,256]{3,2,1,0:T(8,128)(2,1)} %get-tuple-element.11), calls=%async_computation.1 | async-start | bytes 524288 | tf_op jit(solution)/shard_map/all_to_all | solution.py:220
  47.8 0.0 collective-permute-done.1.side_ref
  47.8 0.0 collective-permute-done.2.cross_ref
  47.8 0.0 copy-done.1
  47.8 2.9 %attend.1 = bf16[1280,128]{1,0:T(8,128)(2,1)} custom-call(s32[1]{0:T(128)S(6)} %copy.9.evict_ref, bf16[1024,128]{1,0:T(8,128)(2,1)S(1)} %bitcast.7, bf16[1136,256]{1,0:T(8,128)(2,1)S(1)} %copy-done.1, bf16[1136,256]{1,0:T(8,128)(2,1)S(1)} %collective-permute-done.far_ref, bf16[1136,256]{1,0:T(8,128)(2,1)S(1)} %collective-permute-done.1.side_ref, ...), custom_call_target="tpu_custom_call" | custom-call | tf_op jit(solution)/shard_map/attend/pallas_call | solution.py:212
  50.6 0.0 copy-start
  50.7 8.2 %all-to-all-done.1.near_ref = bf16[16,2,16,256]{3,2,1,0:T(8,128)(2,1)S(1)} async-done(((bf16[16,2,16,256]{3,2,1,0:T(8,128)(2,1)}), bf16[16,2,16,256]{3,2,1,0:T(8,128)(2,1)S(1)}, u32[]{:S(2)}, u32[]{:S(2)}) %all-to-all-start.1) | async-done | bytes 262176 | tf_op jit(solution)/shard_map/all_to_all | solution.py:220
  58.8 8.0 %all-to-all-start.2 = ((bf16[640,2,128]{2,1,0:T(2,128)(2,1)}), bf16[640,2,128]{2,1,0:T(2,128)(2,1)S(1)}, u32[]{:S(2)}, u32[]{:S(2)}) async-start(bf16[640,2,128]{2,1,0:T(2,128)(2,1)} %bitcast.3), calls=%async_computation.2 | async-start | bytes 655360 | tf_op jit(solution)/shard_map/all_to_all | solution.py:222
  66.9 2.5 %collective-permute-start.3 = (bf16[16,2,16,256]{3,2,1,0:T(8,128)(2,1)S(1)}, bf16[16,2,16,256]{3,2,1,0:T(8,128)(2,1)S(1)}, u32[]{:S(2)}, u32[]{:S(2)}) collective-permute-start(bf16[16,2,16,256]{3,2,1,0:T(8,128)(2,1)S(1)} %all-to-all-done.1.near_ref), channel_id=1, source_target_pairs={{0,16},{16,0},{1,17},{17,1},{2,18},{18,2},{3,19},{19,3},{4,20},{20... | collective-permute-start | bytes 786440 | tf_op jit(solution)/shard_map/ppermute | solution.py:232
  69.4 10.2 %collective-permute-done.3.far_ref = bf16[16,2,16,256]{3,2,1,0:T(8,128)(2,1)S(1)} collective-permute-done((bf16[16,2,16,256]{3,2,1,0:T(8,128)(2,1)S(1)}, bf16[16,2,16,256]{3,2,1,0:T(8,128)(2,1)S(1)}, u32[]{:S(2)}, u32[]{:S(2)}) %collective-permute-start.3) | collective-permute-done | bytes 262176 | tf_op jit(solution)/shard_map/ppermute | solution.py:232
  79.6 0.0 copy-done
  79.6 0.8 renew_cache.1
  80.4 2.4 %all-to-all-done.2 = bf16[640,2,128]{2,1,0:T(2,128)(2,1)S(1)} async-done(((bf16[640,2,128]{2,1,0:T(2,128)(2,1)}), bf16[640,2,128]{2,1,0:T(2,128)(2,1)S(1)}, u32[]{:S(2)}, u32[]{:S(2)}) %all-to-all-start.2) | async-done | bytes 327712 | tf_op jit(solution)/shard_map/all_to_all | solution.py:222
  82.8 1.1 %combine.1 = bf16[2,4096]{1,0:T(2,128)(2,1)} custom-call(bf16[1280,128]{1,0:T(8,128)(2,1)S(1)} %bitcast.6), custom_call_target="tpu_custom_call" | custom-call | tf_op jit(solution)/shard_map/combine/pallas_call | solution.py:225
Async XLA Ops:
  4.1 43.7 %copy-start.1 = (bf16[1136,256]{1,0:T(8,128)(2,1)S(1)}, bf16[1136,256]{1,0:T(8,128)(2,1)}, u32[]{:S(2)}) copy-start(bf16[1136,256]{1,0:T(8,128)(2,1)} %get-tuple-element.9.pack_ref) | copy-start | bytes 1744900
  4.1 25.3 %collective-permute-start = (bf16[1136,256]{1,0:T(8,128)(2,1)}, bf16[1136,256]{1,0:T(8,128)(2,1)S(1)}, u32[]{:S(2)}, u32[]{:S(2)}) collective-permute-start(bf16[1136,256]{1,0:T(8,128)(2,1)} %get-tuple-element.9.pack_ref), channel_id=1, source_target_pairs={{0,16},{16,0},{1,17},{17,1},{2,18},{18,2},{3,19},{19,3},{4,20},{20... | collective-permute-start | bytes 1744904 | tf_op jit(solution)/shard_map/ppermute | solution.py:206
  8.5 35.0 %all-to-all-start = ((bf16[128,8,128]{2,1,0:T(8,128)(2,1)}), bf16[128,8,128]{2,1,0:T(8,128)(2,1)S(1)}, u32[]{:S(2)}, u32[]{:S(2)}) async-start(bf16[128,8,128]{2,1,0:T(8,128)(2,1)} %bitcast.8), calls=%async_computation | async-start | bytes 524288 | tf_op jit(solution)/shard_map/all_to_all | solution.py:209
  27.5 20.2 %collective-permute-start.1 = (bf16[1136,256]{1,0:T(8,128)(2,1)}, bf16[1136,256]{1,0:T(8,128)(2,1)S(1)}, u32[]{:S(2)}, u32[]{:S(2)}) collective-permute-start(bf16[1136,256]{1,0:T(8,128)(2,1)} %get-tuple-element.9.pack_ref), channel_id=1, source_target_pairs={{0,1},{1,0},{2,3},{3,2},{4,5},{5,4},{6,7},{7,6},{8,9},{9,8},{10,11... | collective-permute-start | bytes 1744904 | tf_op jit(solution)/shard_map/ppermute | solution.py:207
  29.5 18.3 %collective-permute-start.2 = (bf16[1136,256]{1,0:T(8,128)(2,1)S(1)}, bf16[1136,256]{1,0:T(8,128)(2,1)S(1)}, u32[]{:S(2)}, u32[]{:S(2)}) collective-permute-start(bf16[1136,256]{1,0:T(8,128)(2,1)S(1)} %collective-permute-done.far_ref), channel_id=1, source_target_pairs={{0,1},{1,0},{2,3},{3,2},{4,5},{5,4},{6,7},{7,6},{8,9},{9,8},{10,11... | collective-permute-start | bytes 1744904 | tf_op jit(solution)/shard_map/ppermute | solution.py:208
  43.6 15.3 %all-to-all-start.1 = ((bf16[16,2,16,256]{3,2,1,0:T(8,128)(2,1)}), bf16[16,2,16,256]{3,2,1,0:T(8,128)(2,1)S(1)}, u32[]{:S(2)}, u32[]{:S(2)}) async-start(bf16[16,2,16,256]{3,2,1,0:T(8,128)(2,1)} %get-tuple-element.11), calls=%async_computation.1 | async-start | bytes 524288 | tf_op jit(solution)/shard_map/all_to_all | solution.py:220
  50.6 28.9 %copy-start = (bf16[1,2,512,256]{3,2,1,0:T(8,128)(2,1)S(1)}, bf16[1,2,512,256]{3,2,1,0:T(8,128)(2,1)}, u32[]{:S(2)}) copy-start(bf16[1,2,512,256]{3,2,1,0:T(8,128)(2,1)} %cache_ref.3) | copy-start | bytes 1572868
  58.8 23.9 %all-to-all-start.2 = ((bf16[640,2,128]{2,1,0:T(2,128)(2,1)}), bf16[640,2,128]{2,1,0:T(2,128)(2,1)S(1)}, u32[]{:S(2)}, u32[]{:S(2)}) async-start(bf16[640,2,128]{2,1,0:T(2,128)(2,1)} %bitcast.3), calls=%async_computation.2 | async-start | bytes 655360 | tf_op jit(solution)/shard_map/all_to_all | solution.py:222
  66.9 12.7 %collective-permute-start.3 = (bf16[16,2,16,256]{3,2,1,0:T(8,128)(2,1)S(1)}, bf16[16,2,16,256]{3,2,1,0:T(8,128)(2,1)S(1)}, u32[]{:S(2)}, u32[]{:S(2)}) collective-permute-start(bf16[16,2,16,256]{3,2,1,0:T(8,128)(2,1)S(1)} %all-to-all-done.1.near_ref), channel_id=1, source_target_pairs={{0,16},{16,0},{1,17},{17,1},{2,18},{18,2},{3,19},{19,3},{4,20},{20... | collective-permute-start | bytes 786440 | tf_op jit(solution)/shard_map/ppermute | solution.py:232
